TPU v7x, 256 devices: a whole 4x4x8 slice. The times are simulated.
256 devices in a mesh: dp: 8 (over z_lo, y), tensor: 32 (over z_hi, x, core).
Axes of the slice: x: 4, y: 4, z: 8 (z_hi: 4, z_lo: 2; z = z_hi * 2 + z_lo), core: 2. Of those that a mesh axis runs over, the one named last changes fastest.
Arguments:
- old_master: float32 [32, 8, 128, 2048], P('tensor', 'dp'), may hold values from -6 to 6
- old_moment: float32 [32, 8, 128, 2048], P('tensor', 'dp'), may hold values from -3 to 3
- old_second: float32 [32, 8, 128, 2048], P('tensor', 'dp'), may hold values from 0.25 to 4
- tokens_in: bfloat16 [4096, 4096], P('dp'), may hold values from -6 to 6
- upstream: bfloat16 [4096, 16384], P('dp', 'tensor'), may hold values from -6 to 6
- counts: int32 [8], replicated, may hold values from 128 to 512, as said below
- old_map: int32 [32], replicated, may hold values from 0 to 31, each once
- new_map: int32 [32], replicated, may hold values from 0 to 31, each once
Outputs:
- new_master: float32 [32, 8, 256, 1024], P('tensor', 'dp')
- new_moment: float32 [32, 8, 256, 1024], P('tensor', 'dp')
- new_second: float32 [32, 8, 256, 1024], P('tensor', 'dp')
- input_grad: bfloat16 [4096, 4096], P('dp', 'tensor')
Inputs may be any that keep to these rules, and one draw needn't show every extreme that they name: counts[g] tokens of data group g carry loss, the rest are padding; some group is full in every draw. `old_map`: a permutation of the tensor indices. `new_map`: a permutation of the tensor indices.
All inputs are finite; a program needn't handle non-finite values.
Results may differ from a plain program's by a relative error of at most 0.0049.
Values may be sent and summed in bfloat16 or wider, within the bound.
A program may use at most 128 MiB of HBM per device.

v0:
```python
import jax
import jax.numpy as jnp
from jax import lax
from jax.sharding import PartitionSpec as P

beta_first = 0.9
beta_second = 0.95
learn_rate = 0.05
decay_rate = 0.1
epsilon = 1e-08


def shards(old_master, old_moment, old_second, tokens_in, upstream, counts, old_map, new_map):
    lanes = lax.axis_size("tensor")
    groups = lax.axis_size("dp")
    rows_old = old_master.shape[2]
    cols_old = old_master.shape[3]
    cols_new = cols_old // 2
    tok_count = tokens_in.shape[0]
    width = tokens_in.shape[1]
    atom_cols = upstream.shape[1]
    r_new = lanes // 16
    slab = rows_old // lanes
    token_slab = tok_count // lanes
    rows_new = 2 * rows_old
    shard_ids = jnp.arange(lanes, dtype=jnp.int32)
    here = lax.axis_index("tensor")
    group = lax.axis_index("dp")
    inverse = jnp.sum(
        jnp.where(old_map[None, :] == shard_ids[:, None], shard_ids[None, :], 0), axis=1
    )

    def outgoing(stored):
        return stored.reshape(lanes, slab, cols_old)

    recv_master, recv_moment, recv_second, recv_tokens = (
        lax.all_to_all(outgoing(old_master), "tensor", split_axis=0, concat_axis=0, tiled=True),
        lax.all_to_all(outgoing(old_moment), "tensor", split_axis=0, concat_axis=0, tiled=True),
        lax.all_to_all(outgoing(old_second), "tensor", split_axis=0, concat_axis=0, tiled=True),
        lax.all_to_all(
            upstream.reshape(lanes, token_slab, atom_cols).astype(jnp.float32),
            "tensor",
            split_axis=0,
            concat_axis=0,
            tiled=True,
        ).astype(jnp.bfloat16),
    )

    def arrange(received):
        ordered = jnp.take(received, inverse, axis=0).reshape(8, r_new, 2, slab, 2, cols_new)
        ordered = ordered.transpose(0, 4, 1, 2, 3, 5).reshape(lanes, 2, slab, cols_new)
        return jnp.take(ordered, new_map, axis=0)

    blocks = recv_tokens.reshape(16, r_new, token_slab, atom_cols).transpose(0, 2, 1, 3)
    blocks = blocks.reshape(16, token_slab, cols_new)
    token_send = jnp.take(blocks, new_map // r_new, axis=0)
    got_master, got_moment, got_second, got_tokens = (
        lax.all_to_all(arrange(recv_master), "tensor", split_axis=0, concat_axis=0, tiled=True),
        lax.all_to_all(arrange(recv_moment), "tensor", split_axis=0, concat_axis=0, tiled=True),
        lax.all_to_all(arrange(recv_second), "tensor", split_axis=0, concat_axis=0, tiled=True),
        lax.all_to_all(
            token_send.astype(jnp.float32), "tensor", split_axis=0, concat_axis=0, tiled=True
        ).astype(token_send.dtype),
    )

    def settle(received):
        return received.transpose(1, 0, 2, 3).reshape(rows_new, cols_new)

    master = settle(got_master)
    moment_old = settle(got_moment)
    second_old = settle(got_second)
    grad_block = got_tokens.reshape(tok_count, cols_new)
    own_shard = jnp.sum(jnp.where(shard_ids == here, new_map, 0))
    row_part = own_shard % r_new
    live_count = jnp.sum(jnp.where(jnp.arange(groups, dtype=jnp.int32) == group, counts, 0))
    live = jnp.arange(tok_count, dtype=jnp.int32) < live_count
    masked = jnp.where(live[:, None], grad_block, jnp.zeros_like(grad_block))
    scale = float(width) ** (-0.5)
    selected = lax.dynamic_index_in_dim(
        tokens_in.reshape(tok_count, groups, r_new, rows_new), row_part, axis=2, keepdims=False
    )
    selected = selected.reshape(tok_count, groups * rows_new)
    summed = lax.psum(
        (
            lax.dot_general(
                selected, masked, (((0,), (0,)), ((), ())), preferred_element_type=jnp.float32
            )
            * scale
        ).astype(jnp.bfloat16),
        "dp",
    ).astype(jnp.float32)
    grad = lax.dynamic_slice_in_dim(summed, group * rows_new, rows_new, 0)
    weights = master.astype(jnp.bfloat16)
    partial_grad = (
        lax.dot_general(
            masked,
            lax.all_gather(weights, "dp", axis=0, tiled=True),
            (((1,), (1,)), ((), ())),
            preferred_element_type=jnp.float32,
        )
        * scale
    )
    placing = (jnp.arange(r_new, dtype=jnp.int32) == row_part).astype(jnp.float32)
    spread = partial_grad.reshape(tok_count, groups, 1, rows_new) * placing.reshape(1, 1, r_new, 1)
    input_grad = lax.psum_scatter(
        spread.reshape(tok_count, width), "tensor", scatter_dimension=1, tiled=True
    ).astype(jnp.bfloat16)
    moment = beta_first * moment_old + (1.0 - beta_first) * grad
    second = beta_second * second_old + (1.0 - beta_second) * grad * grad
    fix_first = 1.0 - beta_first**10
    fix_second = 1.0 - beta_second**10
    update = moment / fix_first / (jnp.sqrt(second / fix_second) + epsilon) + decay_rate * master
    updated = master - learn_rate * update
    shape_out = (1, 1, rows_new, cols_new)
    return (
        updated.reshape(shape_out),
        moment.reshape(shape_out),
        second.reshape(shape_out),
        input_grad,
    )


def solution(mesh):
    placed = (
        P("tensor", "dp", None, None),
        P("tensor", "dp", None, None),
        P("tensor", "dp", None, None),
        P("dp", None),
        P("dp", "tensor"),
        P(),
        P(),
        P(),
    )
    return jax.shard_map(
        shards,
        mesh=mesh,
        in_specs=placed,
        out_specs=(
            P("tensor", "dp", None, None),
            P("tensor", "dp", None, None),
            P("tensor", "dp", None, None),
            P("dp", "tensor"),
        ),
        check_vma=False,
    )
```

profile of v0, /device:TPU:1, one launch (start us, length us, event | category | flops | bytes accessed | tf_op | source)
XLA Modules:
  0.0 588.2 jit_solution(6907345303401353057)
XLA Ops:
  7.2 12.7 %all-to-all-start.4 = ((bf16[32,16,512]{2,1,0:T(8,128)(2,1)}), bf16[32,16,512]{2,1,0:T(8,128)(2,1)S(1)}, u32[]{:S(2)}, u32[]{:S(2)}) async-start(bf16[32,16,512]{2,1,0:T(8,128)(2,1)} %bitcast.61), calls=%async_computation.4 | async-start | bytes 1048576 | tf_op jit(solution)/shard_map/all_to_all | solution.py:40
  19.9 2.5 reshape.121
  22.4 15.5 %all-to-all-done.4 = bf16[32,16,512]{2,1,0:T(8,128)(2,1)S(1)} async-done(((bf16[32,16,512]{2,1,0:T(8,128)(2,1)}), bf16[32,16,512]{2,1,0:T(8,128)(2,1)S(1)}, u32[]{:S(2)}, u32[]{:S(2)}) %all-to-all-start.4) | async-done | bytes 524320 | tf_op jit(solution)/shard_map/all_to_all | solution.py:40
  37.9 4.5 all-to-all-start.6
  42.5 1.3 reshape.114
  43.7 27.4 %all-to-all-done.6 = f32[32,4,2048]{2,1,0:T(4,128)S(1)} async-done(((f32[32,4,2048]{2,1,0:T(4,128)}), f32[32,4,2048]{2,1,0:T(4,128)S(1)}, u32[]{:S(2)}, u32[]{:S(2)}) %all-to-all-start.6) | async-done | bytes 1048608 | tf_op jit(solution)/shard_map/all_to_all | solution.py:39
  71.2 5.6 all-to-all-start.2
  76.8 2.5 reshape.110
  79.3 26.2 %all-to-all-done.2 = f32[32,4,2048]{2,1,0:T(4,128)S(1)} async-done(((f32[32,4,2048]{2,1,0:T(4,128)}), f32[32,4,2048]{2,1,0:T(4,128)S(1)}, u32[]{:S(2)}, u32[]{:S(2)}) %all-to-all-start.2) | async-done | bytes 1048608 | tf_op jit(solution)/shard_map/all_to_all | solution.py:38
  105.4 5.7 all-to-all-start
  113.0 26.8 %all-to-all-done = f32[32,4,2048]{2,1,0:T(4,128)} async-done(((f32[32,4,2048]{2,1,0:T(4,128)}), f32[32,4,2048]{2,1,0:T(4,128)}, u32[]{:S(2)}, u32[]{:S(2)}) %all-to-all-start) | async-done | bytes 1048608 | tf_op jit(solution)/shard_map/all_to_all | solution.py:37
  139.8 5.3 all-to-all-start.5
  145.9 1.2 gather_fusion.5
  147.1 2.4 gather_fusion.3
  149.5 3.3 gather_fusion.1
  152.8 3.6 broadcast_select_fusion.4
  156.5 3.4 reshape.206
  159.8 1.6 copy.43
  161.4 2.0 reshape.205
  163.5 2.6 copy.38
  167.3 2.4 gather_fusion.4
  169.7 3.3 reshape.204
  172.9 2.6 copy.35
  175.5 3.3 gather_fusion.2
  178.8 3.7 broadcast_select_fusion.1
  182.5 9.8 %all-to-all-start.7 = ((f32[32,2,4,1024]{3,2,1,0:T(4,128)}), f32[32,2,4,1024]{3,2,1,0:T(4,128)S(1)}, u32[]{:S(2)}, u32[]{:S(2)}) async-start(f32[32,2,4,1024]{3,2,1,0:T(4,128)} %get-tuple-element.15), calls=%async_computation.7 | async-start | bytes 2097152 | tf_op jit(solution)/shard_map/all_to_all | solution.py:60
  194.3 6.5 %copy.40 = bf16[512,4096]{0,1:T(8,128)(2,1)} copy(bf16[512,4096]{1,0:T(8,128)(2,1)} %param.15) | data formatting | bytes 8388608 | tf_op args[3]
  202.1 3.1 constant_dynamic-slice_fusion
  206.3 14.7 %all-to-all-done.7 = f32[32,2,4,1024]{3,2,1,0:T(4,128)S(1)} async-done(((f32[32,2,4,1024]{3,2,1,0:T(4,128)}), f32[32,2,4,1024]{3,2,1,0:T(4,128)S(1)}, u32[]{:S(2)}, u32[]{:S(2)}) %all-to-all-start.7) | async-done | bytes 1048608 | tf_op jit(solution)/shard_map/all_to_all | solution.py:60
  220.9 5.3 all-to-all-start.1
  226.3 6.1 %multiply_convert_fusion = bf16[2048,1024]{1,0:T(8,128)(2,1)} fusion(bf16[512,2048]{0,1:T(8,128)(2,1)} %bitcast.58, bf16[512,1024]{1,0:T(8,128)(2,1)} %bitcast.60), kind=kOutput, calls=%fused_computation.7 | convolution fusion | flops 2151677952 | bytes 7340032 | tf_op jit(solution)/shard_map/dot_general | solution.py:85
  232.4 24.7 %all-to-all-done.1 = f32[32,2,4,1024]{3,2,1,0:T(4,128)S(1)} async-done(((f32[32,2,4,1024]{3,2,1,0:T(4,128)}), f32[32,2,4,1024]{3,2,1,0:T(4,128)S(1)}, u32[]{:S(2)}, u32[]{:S(2)}) %all-to-all-start.1) | async-done | bytes 1048608 | tf_op jit(solution)/shard_map/all_to_all | solution.py:58
  257.1 5.9 all-to-all-start.3
  263.6 1.3 mul.87
  265.0 1.3 reshape.113
  266.3 33.1 %all-to-all-done.3 = f32[32,2,4,1024]{3,2,1,0:T(4,128)} async-done(((f32[32,2,4,1024]{3,2,1,0:T(4,128)}), f32[32,2,4,1024]{3,2,1,0:T(4,128)}, u32[]{:S(2)}, u32[]{:S(2)}) %all-to-all-start.3) | async-done | bytes 1048608 | tf_op jit(solution)/shard_map/all_to_all | solution.py:59
  299.4 1.6 multiply_bitcast_fusion.1
  301.1 1.3 mul.79
  302.4 67.3 %all-reduce.2.cloned.1.call-done = bf16[2048,1024]{1,0:T(8,128)(2,1)} async-done(((bf16[2048,1024]{1,0:T(8,128)(2,1)}), bf16[2048,1024]{1,0:T(8,128)(2,1)}) %all-reduce.2.cloned.1.call-update) | async-done | bytes 4194320 | tf_op jit(solution)/shard_map/psum | solution.py:83
  369.7 4.7 fusion.3
  375.4 53.2 %all-gather.2.cloned.1.call-done = bf16[2048,1024]{1,0:T(8,128)(2,1)} async-done(((bf16[256,1024]{1,0:T(8,128)(2,1)}), bf16[2048,1024]{1,0:T(8,128)(2,1)}) %all-gather.2.cloned.1.call-update) | async-done | bytes 4194320 | tf_op jit(solution)/shard_map/all_gather | solution.py:97
  428.6 4.6 convolution_multiply_fusion
  433.2 2.0 copy.52
  435.1 6.0 %mul.95 = f32[512,8,2,256]{3,2,1,0:T(2,128)} broadcast(f32[512,8,256]{2,1,0:T(8,128)S(1)} %bitcast.47), dimensions={0,1,3} | broadcast | bytes 12582912 | tf_op jit(solution)/shard_map/mul | solution.py:104
  441.1 11.5 %mul.96 = f32[512,4096]{1,0:T(8,128)} reshape(f32[512,8,2,256]{3,2,1,0:T(2,128)} %mul.95) | data formatting | bytes 16777216 | tf_op jit(solution)/shard_map/mul | solution.py:104
  452.6 7.9 %broadcast_multiply_fusion = f32[512,4096]{1,0:T(8,128)} fusion(f32[512,4096]{1,0:T(8,128)} %mul.96, f32[4096]{0:T(1024)S(1)} %bitcast.62), kind=kLoop, calls=%fused_computation.8 | loop fusion | flops 2097152 | bytes 16793600 | tf_op jit(solution)/shard_map/mul | solution.py:104
  460.6 119.5 %reduce-scatter.2.cloned.1.call-done = f32[512,128]{1,0:T(8,128)} async-done(((f32[512,4096]{1,0:T(8,128)}), f32[512,128]{1,0:T(8,128)}) %reduce-scatter.2.cloned.1.call-update) | async-done | bytes 262160 | tf_op jit(solution)/shard_map/reduce_scatter | solution.py:105
  580.0 1.6 convert_element_type.43
  (45 shorter events, 8.0 us)
Async XLA Ops:
  7.2 35.3 %copy-start.3 = (f32[1,1,128,2048]{3,2,1,0:T(8,128)S(1)}, f32[1,1,128,2048]{3,2,1,0:T(8,128)}, u32[]{:S(2)}) copy-start(f32[1,1,128,2048]{3,2,1,0:T(8,128)} %param.13) | copy-start | bytes 3145732
  7.2 30.8 %all-to-all-start.4 = ((bf16[32,16,512]{2,1,0:T(8,128)(2,1)}), bf16[32,16,512]{2,1,0:T(8,128)(2,1)S(1)}, u32[]{:S(2)}, u32[]{:S(2)}) async-start(bf16[32,16,512]{2,1,0:T(8,128)(2,1)} %bitcast.61), calls=%async_computation.4 | async-start | bytes 1048576 | tf_op jit(solution)/shard_map/all_to_all | solution.py:40
  37.9 33.2 %all-to-all-start.6 = ((f32[32,4,2048]{2,1,0:T(4,128)}), f32[32,4,2048]{2,1,0:T(4,128)S(1)}, u32[]{:S(2)}, u32[]{:S(2)}) async-start(f32[32,4,2048]{2,1,0:T(4,128)} %reshape.121), calls=%async_computation.6 | async-start | bytes 2097152 | tf_op jit(solution)/shard_map/all_to_all | solution.py:39
  42.4 68.7 %copy-start.4 = (s32[32]{0:T(128)S(1)}, s32[32]{0:T(128)}, u32[]{:S(2)}) copy-start(s32[32]{0:T(128)} %param.19) | copy-start | bytes 388
  71.2 34.3 %all-to-all-start.2 = ((f32[32,4,2048]{2,1,0:T(4,128)}), f32[32,4,2048]{2,1,0:T(4,128)S(1)}, u32[]{:S(2)}, u32[]{:S(2)}) async-start(f32[32,4,2048]{2,1,0:T(4,128)} %reshape.114), calls=%async_computation.2 | async-start | bytes 2097152 | tf_op jit(solution)/shard_map/all_to_all | solution.py:38
  105.4 5.7 copy-start.1
  105.4 34.4 %all-to-all-start = ((f32[32,4,2048]{2,1,0:T(4,128)}), f32[32,4,2048]{2,1,0:T(4,128)}, u32[]{:S(2)}, u32[]{:S(2)}) async-start(f32[32,4,2048]{2,1,0:T(4,128)} %reshape.110), calls=%async_computation | async-start | bytes 2097152 | tf_op jit(solution)/shard_map/all_to_all | solution.py:37
  111.1 34.0 %copy-start.5 = (s32[32]{0:T(128)S(1)}, s32[32]{0:T(128)}, u32[]{:S(2)}) copy-start(s32[32]{0:T(128)} %param.18) | copy-start | bytes 388
  139.8 42.7 %all-to-all-start.5 = ((bf16[32,16,1024]{2,1,0:T(8,128)(2,1)}), bf16[32,16,1024]{2,1,0:T(8,128)(2,1)S(1)}, u32[]{:S(2)}, u32[]{:S(2)}) async-start(bf16[32,16,1024]{2,1,0:T(8,128)(2,1)} %select_convert_fusion), calls=%async_computation.5 | async-start | bytes 2097152 | tf_op jit(solution)/shard_map/all_to_all | solution.py:61
  156.4 5.0 copy-start
  182.5 38.4 %all-to-all-start.7 = ((f32[32,2,4,1024]{3,2,1,0:T(4,128)}), f32[32,2,4,1024]{3,2,1,0:T(4,128)S(1)}, u32[]{:S(2)}, u32[]{:S(2)}) async-start(f32[32,2,4,1024]{3,2,1,0:T(4,128)} %get-tuple-element.15), calls=%async_computation.7 | async-start | bytes 2097152 | tf_op jit(solution)/shard_map/all_to_all | solution.py:60
  194.3 6.5 %copy-start.6 = (s32[8]{0:T(128)S(1)}, s32[8]{0:T(128)}, u32[]{:S(2)}) copy-start(s32[8]{0:T(128)} %param.17) | copy-start | bytes 100
  220.9 36.2 %all-to-all-start.1 = ((f32[32,2,4,1024]{3,2,1,0:T(4,128)}), f32[32,2,4,1024]{3,2,1,0:T(4,128)S(1)}, u32[]{:S(2)}, u32[]{:S(2)}) async-start(f32[32,2,4,1024]{3,2,1,0:T(4,128)} %get-tuple-element.17), calls=%async_computation.1 | async-start | bytes 2097152 | tf_op jit(solution)/shard_map/all_to_all | solution.py:58
  226.2 143.5 %all-reduce.2.cloned.1.call-start = ((), (), s32[]{:S(2)}) async-start(), calls=%async_computation.9 | async-start | bytes 8388608 | tf_op jit(solution)/shard_map/psum | solution.py:83
  257.1 42.3 %all-to-all-start.3 = ((f32[32,2,4,1024]{3,2,1,0:T(4,128)}), f32[32,2,4,1024]{3,2,1,0:T(4,128)}, u32[]{:S(2)}, u32[]{:S(2)}) async-start(f32[32,2,4,1024]{3,2,1,0:T(4,128)} %get-tuple-element.16), calls=%async_computation.3 | async-start | bytes 2097152 | tf_op jit(solution)/shard_map/all_to_all | solution.py:59
  263.0 165.6 %all-gather.2.cloned.1.call-start = ((), (), s32[]{:S(2)}) async-start(), calls=%async_computation.10 | async-start | bytes 4718592 | tf_op jit(solution)/shard_map/all_gather | solution.py:97
  265.0 104.7 %copy-start.2 = (f32[256,1024]{1,0:T(8,128)S(1)}, f32[256,1024]{1,0:T(8,128)}, u32[]{:S(2)}) copy-start(f32[256,1024]{1,0:T(8,128)} %mul.87) | copy-start | bytes 3145732
  374.4 205.6 %reduce-scatter.2.cloned.1.call-start = ((), (), s32[]{:S(2)}) async-start(), calls=%async_computation.11 | async-start | bytes 8650752 | tf_op jit(solution)/shard_map/reduce_scatter | solution.py:105
Sparse Core Ops, SparseCore 0:
  232.6 137.0 all-reduce.1
  374.5 54.0 all-gather.1
  460.7 119.2 reduce-scatter.1
where the time goes:
time: 590 us; the launch traced here: 588 us
  waiting for transfers between devices  408 us (69%)
  local copies, waits for them, and re-layouts  69.5 us (12%)
  starting transfers between devices  54.8 us (9%)
  other arithmetic  28.7 us (5%)
  between operations  16 us (3%)
  matrix products  10.7 us (2%)
    reduce_scatter x1, waiting for transfers between devices, shards(): lax.psum_scatter(spread.reshape(tok_count, width), 'tensor', scatter_dime...  119 us
    psum x1, waiting for transfers between devices, shards(): lax.psum((lax.dot_general(selected, masked, (((0,), (0,)), ((), ())), pre...  67.3 us
    all_gather x1, waiting for transfers between devices, shards(): lax.all_gather(weights, 'dp', axis=0, tiled=True)  53.2 us
    all_to_all x1, waiting for transfers between devices, shards(): lax.all_to_all(arrange(recv_moment), 'tensor', split_axis=0, concat_axis=...  33.1 us
    all_to_all x1, waiting for transfers between devices, shards(): lax.all_to_all(outgoing(old_second), 'tensor', split_axis=0, concat_axis=...  27.4 us
    all_to_all x1, waiting for transfers between devices, shards(): lax.all_to_all(outgoing(old_master), 'tensor', split_axis=0, concat_axis=...  26.8 us
    all_to_all x1, waiting for transfers between devices, shards(): lax.all_to_all(outgoing(old_moment), 'tensor', split_axis=0, concat_axis=...  26.2 us
    all_to_all x1, waiting for transfers between devices, shards(): lax.all_to_all(arrange(recv_master), 'tensor', split_axis=0, concat_axis=...  24.7 us
  transfers between devices with their start and end apart: 11, of which 10 were waited for; matrix products, arithmetic and copies ran while one was open for 12% of the time, Pallas kernels for 0%

commit v1 on v0

v1 whole, which is shorter than its diff:
```python
import jax
import jax.numpy as jnp
from jax import lax
from jax.experimental import pallas as pl
from jax.experimental.pallas import tpu as pltpu
from jax.sharding import PartitionSpec as P

beta_first = 0.9
beta_second = 0.95
learn_rate = 0.05
decay_rate = 0.1
epsilon = 1e-08

BF = jnp.bfloat16
F32 = jnp.float32
NT = (((1,), (1,)), ((), ()))


def kernel(
    inv_ref, new_ref, cnt_ref, om_ref, oo_ref, os_ref, tok_ref, up_ref,
    out_ref, ig_ref,
    old, tok, send1, spread_a, spread_b, spread_c, gath, lhs, part, r1, r2, r3, qsend, wg,
    upd, send2, cpart, crecv, csum, cfin,
    ld, us, ur, p1s, p1r, xs, xr, ws, wr, rs, rr, p2s, p2r, cs, cr,
):
    spread = (spread_a, spread_b, spread_c)
    g = lax.axis_index("dp")
    t = lax.axis_index("tensor")
    zl, y = g // 4, g % 4
    z, x, k = t // 8, (t // 2) % 4, t % 2
    zp = 1 - zl
    y_up, y_dn, y_far = (y + 1) % 4, (y + 3) % 4, (y + 2) % 4
    g_up, g_dn, g_pair = zl * 4 + y_up, zl * 4 + y_dn, zp * 4 + y
    x_up, x_dn = (x + 1) % 4, (x + 3) % 4
    t_xup, t_xdn = z * 8 + x_up * 2 + k, z * 8 + x_dn * 2 + k
    x_far = (x + 2) % 4
    t_core = z * 8 + x * 2 + 1 - k

    def remote(src, dst, ssem, rsem, dp, tn):
        return pltpu.make_async_remote_copy(
            src_ref=src, dst_ref=dst, send_sem=ssem, recv_sem=rsem,
            device_id=(dp, tn), device_id_type=pl.DeviceIdType.MESH,
        )

    def cols(index, width):
        return pl.ds(pl.multiple_of(index * width, width), width)

    loads = [
        pltpu.make_async_copy(src, old.at[a], ld.at[a]) for a, src in enumerate((om_ref, oo_ref, os_ref))
    ] + [pltpu.make_async_copy(tok_ref, tok, ld.at[3])]
    for c in loads:
        c.start()

    barrier = pltpu.get_barrier_semaphore()

    def greet(j, c):
        pl.semaphore_signal(barrier, inc=1, device_id=(g, (t + j) % 32), device_id_type=pl.DeviceIdType.MESH)
        return c

    lax.fori_loop(1, 32, greet, 0)
    for other in (g_up, g_dn, g_pair):
        pl.semaphore_signal(barrier, inc=1, device_id=(other, t), device_id_type=pl.DeviceIdType.MESH)

    def narrow(a):
        loads[a].wait()

        def body(i, c):
            c10, xx = i // 4, i % 4
            send1[a, c10, xx] = old[a, cols(xx, 32), cols(c10, 1024)].astype(BF)
            return c

        lax.fori_loop(0, 8, body, 0)

    narrow(0)
    pl.semaphore_wait(barrier, 34)

    def u1(dz):
        to = (z + dz) % 4
        return remote(
            up_ref.at[:, cols(to, 128)], gath.at[:, cols(x * 4 + z, 128)],
            us.at[dz], ur.at[dz], g, to * 8 + x * 2 + k,
        )

    def u1_in(dz):
        of = (z + 4 - dz) % 4
        return remote(
            up_ref.at[:, cols(z, 128)], gath.at[:, cols(x * 4 + of, 128)],
            us.at[dz], ur.at[dz], g, t_core,
        )

    u1_own = pltpu.make_async_copy(up_ref.at[:, cols(z, 128)], gath.at[:, cols(x * 4 + z, 128)], ur.at[0])
    u1_own.start()
    for dz in (2, 1, 3):
        u1(dz).start()

    def p1(a, j):
        p = (t + j) % 32
        pz, px, pk = p // 8, (p // 2) % 4, p % 2
        return remote(
            send1.at[a, :, px, :, cols(pk * 4 + pz, 128)], spread[a].at[t],
            p1s.at[a, j], p1r.at[a, j], g, p,
        )

    def p1_in(a, j):
        return remote(
            send1.at[a, :, x, :, cols(k * 4 + z, 128)], spread[a].at[(t + 32 - j) % 32],
            p1s.at[a, j], p1r.at[a, j], g, t_core,
        )

    def p1_own(a):
        return pltpu.make_async_copy(send1.at[a, :, x, :, cols(k * 4 + z, 128)], spread[a].at[t], p1r.at[a, 0])

    def p1_start(a):
        p1_own(a).start()

        def body(j, c):
            p1(a, j).start()
            return c

        lax.fori_loop(1, 32, body, 0)

    def p1_wait(a):
        p1_own(a).wait()

        def body(j, c):
            p1_in(a, j).wait_recv()
            return c

        lax.fori_loop(1, 32, body, 0)

    p1_start(0)
    narrow(1)
    narrow(2)

    loads[3].wait()
    live = cnt_ref[g]
    pick_row = lax.broadcasted_iota(jnp.int32, (128, 512), 0)
    pick_col = lax.broadcasted_iota(jnp.int32, (128, 512), 1)
    pick = jnp.where(pick_col == (pick_row // 32) * 128 + x * 32 + pick_row % 32, 1.0, 0.0).astype(BF)
    alive = lax.broadcasted_iota(jnp.int32, (128, 512), 1) < live

    def transpose_tokens(d, c):
        rows = lax.dot_general(pick, tok[:, cols(d, 512)], NT, preferred_element_type=F32)
        lhs[d % 4, cols(d // 4, 128), :] = jnp.where(alive, rows, 0.0).astype(BF)
        return c

    lax.fori_loop(0, 8, transpose_tokens, 0)

    def ring_x(block, rows, way, sem):
        ref = gath.at[rows, cols(block, 512)]
        return remote(ref, ref, xs.at[sem], xr.at[sem], g, way)

    top, bottom, whole = pl.ds(0, 256), pl.ds(256, 256), pl.ds(0, 512)
    u1_own.wait()
    for dz in (1, 2, 3):
        u1_in(dz).wait_recv()
    x_sends = [ring_x(x, whole, t_xup, 0), ring_x(x, whole, t_xdn, 1)]
    for c in x_sends:
        c.start()

    def place(q, body):
        zs, half = q % 4, q // 4
        bo, c10 = zs * 2 + half // 2, half % 2
        for so in range(4):
            body(so, bo, c10)

    def weights(q, c):
        def one(so, bo, c10):
            wg[y, pl.ds(pl.multiple_of(zl * 128 + so * 32, 32), 32), cols(q, 128)] = spread[0][inv_ref[bo * 4 + so], c10]

        place(q, one)
        return c

    def ring_w(yy, zz, to, sem):
        ref = wg.at[yy, cols(zz, 128), :]
        return remote(ref, ref, ws.at[sem], wr.at[sem], to, t)

    p1_wait(0)
    lax.fori_loop(0, 16, weights, 0)
    w_sends = [ring_w(y, zl, g_pair, 2), ring_w(y, zl, g_up, 0), ring_w(y, zl, g_dn, 1)]
    for c in w_sends:
        c.start()
    p1_start(1)
    p1_start(2)

    ring_x(x_dn, whole, t_xup, 0).wait_recv()
    x_sends.append(ring_x(x_dn, top, t_xup, 2))
    x_sends[-1].start()
    ring_x(x_up, whole, t_xdn, 1).wait_recv()
    x_sends.append(ring_x(x_up, bottom, t_xdn, 3))
    x_sends[-1].start()
    ring_x(x_far, top, t_xup, 2).wait_recv()
    ring_x(x_far, bottom, t_xdn, 3).wait_recv()

    def partial(yy):
        def body(c, carry):
            part[yy, :, cols(c, 512)] = jnp.dot(
                lhs[yy], gath[:, cols(c, 512)], preferred_element_type=F32
            ).astype(BF)
            return carry

        lax.fori_loop(0, 4, body, 0)

    def half_of(ref, yy, zz):
        return ref.at[yy, cols(zz, 128), :]

    partial(y_far)
    r_sends = [
        remote(half_of(part, y_far, 0), r1.at[0], rs.at[0], rr.at[0], g_up, t),
        remote(half_of(part, y_far, 1), r1.at[1], rs.at[1], rr.at[1], g_dn, t),
    ]
    for c in r_sends:
        c.start()
    partial(y_up)
    r_sends.append(remote(half_of(part, y_up, 1), half_of(r2, 0, 1), rs.at[2], rr.at[2], g_up, t))
    r_sends[-1].start()
    partial(y_dn)
    r_sends.append(remote(half_of(part, y_dn, 0), half_of(r2, 1, 0), rs.at[3], rr.at[3], g_dn, t))
    r_sends[-1].start()

    ring_w(y, zp, g_pair, 2).wait_recv()
    w_sends += [ring_w(y, zp, g_up, 3), ring_w(y, zp, g_dn, 4)]
    w_sends[-2].start()
    w_sends[-1].start()
    partial(y)

    def add_into(yy, zz, side):
        def body(c, carry):
            at = (yy, cols(zz, 128), cols(c, 512))
            part[at] = (part[at].astype(F32) + r1[side, :, cols(c, 512)].astype(F32)).astype(BF)
            return carry

        lax.fori_loop(0, 4, body, 0)

    r_sends[0].wait_recv()
    add_into(y_up, 0, 0)
    r_sends.append(remote(half_of(part, y_up, 0), half_of(r2, 0, 0), rs.at[4], rr.at[4], g_up, t))
    r_sends[-1].start()
    r_sends[1].wait_recv()
    add_into(y_dn, 1, 1)
    r_sends.append(remote(half_of(part, y_dn, 1), half_of(r2, 1, 1), rs.at[5], rr.at[5], g_dn, t))
    r_sends[-1].start()

    ring_w(y_dn, zl, g_up, 0).wait_recv()
    ring_w(y_dn, zp, g_up, 3).wait_recv()
    w_sends.append(ring_w(y_dn, 0, g_up, 5))
    w_sends[-1].start()
    ring_w(y_up, zl, g_dn, 1).wait_recv()
    ring_w(y_up, zp, g_dn, 4).wait_recv()
    w_sends.append(ring_w(y_up, 1, g_dn, 6))
    w_sends[-1].start()

    def back(yy):
        block = lax.dot_general(wg[yy], gath[...], NT, preferred_element_type=F32).astype(BF)
        for zz in range(2):
            for so in range(4):
                at = zz * 128 + so * 32
                cpart[zz * 4 + yy, so // 2, so % 2] = block[at : at + 32]

    back(y)
    back(y_dn)
    back(y_up)

    def sum_y(zz, c):
        at = (cols(zz, 128), cols(c, 512))
        total = part[(y, *at)].astype(F32) + r2[(0, *at)].astype(F32)
        return total + r2[(1, *at)].astype(F32)

    for s in (2, 3, 4, 5):
        r_sends[s].wait_recv()

    def for_pair(c, carry):
        qsend[:, cols(c, 512)] = sum_y(zp, c).astype(BF)
        return carry

    lax.fori_loop(0, 4, for_pair, 0)
    r_sends.append(remote(qsend, r3, rs.at[6], rr.at[6], g_pair, t))
    r_sends[-1].start()

    ring_w(y_far, 0, g_up, 5).wait_recv()
    ring_w(y_far, 1, g_dn, 6).wait_recv()
    back(y_far)
    core_send = remote(cpart.at[:, :, 1 - k], crecv, cs.at[0], cr.at[0], g, t_core)
    core_send.start()

    p1_wait(1)
    p1_wait(2)
    r_sends[6].wait_recv()
    fix_first = 1.0 - beta_first**10
    fix_second = 1.0 - beta_second**10
    scale = 1.0 / 64.0

    def step(q, carry):
        def one(so, bo, c10):
            slot = inv_ref[bo * 4 + so]
            here = cols(q, 128)
            at = pl.ds(pl.multiple_of(zl * 128 + so * 32, 32), 32)
            grad = part[y, at, here].astype(F32) + r2[0, at, here].astype(F32)
            grad = grad + r2[1, at, here].astype(F32) + r3[so * 32 : so * 32 + 32, here].astype(F32)
            grad = grad * scale
            master = spread[0][slot, c10].astype(F32)
            moment = beta_first * spread[1][slot, c10].astype(F32) + (1.0 - beta_first) * grad
            second = beta_second * spread[2][slot, c10].astype(F32) + (1.0 - beta_second) * grad * grad
            update = moment / fix_first / (jnp.sqrt(second / fix_second) + epsilon) + decay_rate * master
            piece = (bo * 2 + c10) * 2 + so // 2
            upd[piece, 0, so % 2] = (master - learn_rate * update).astype(BF)
            upd[piece, 1, so % 2] = moment.astype(BF)
            upd[piece, 2, so % 2] = second.astype(BF)

        place(q, one)
        return carry

    lax.fori_loop(0, 16, step, 0)

    def p2(j):
        p = (t + j) % 32
        return remote(
            send2.at[p], out_ref.at[:, :, x, :, cols(k * 4 + z, 128)], p2s.at[j], p2r.at[j], g, p
        )

    def p2_in(j):
        p = (t + 32 - j) % 32
        pz, px, pk = p // 8, (p // 2) % 4, p % 2
        return remote(
            send2.at[t], out_ref.at[:, :, px, :, cols(pk * 4 + pz, 128)], p2s.at[j], p2r.at[j], g, t_core
        )

    def p2_start(j, carry):
        p = (t + j) % 32
        send2[p] = upd[new_ref[p]]
        p2(j).start()
        return carry

    lax.fori_loop(1, 32, p2_start, 0)
    send2[t] = upd[new_ref[t]]
    p2_own = pltpu.make_async_copy(send2.at[t], out_ref.at[:, :, x, :, cols(k * 4 + z, 128)], p2r.at[0])
    p2_own.start()

    core_send.wait_recv()

    def add_core(d, carry):
        csum[d] = (cpart[d, :, k].astype(F32) + crecv[d].astype(F32)).astype(BF)
        return carry

    lax.fori_loop(0, 8, add_core, 0)
    me16 = z * 4 + x

    def c_out(j):
        p = (me16 + j) % 16
        return remote(csum.at[p // 2, p % 2], cfin.at[me16], cs.at[j], cr.at[j], g, p * 2 + k)

    def c_in(j):
        return remote(csum.at[0, 0], cfin.at[(me16 + 16 - j) % 16], cs.at[j], cr.at[j], g, t_core)

    core_send.wait_send()
    c_own = pltpu.make_async_copy(csum.at[me16 // 2, me16 % 2], cfin.at[me16], cr.at[0])
    c_own.start()

    def c_start(j, carry):
        c_out(j).start()
        return carry

    lax.fori_loop(1, 16, c_start, 0)
    c_own.wait()

    def c_wait(j, carry):
        c_in(j).wait_recv()
        return carry

    lax.fori_loop(1, 16, c_wait, 0)
    token = lax.broadcasted_iota(jnp.int32, (512, 128), 0)
    blocks = []
    for xx in range(4):
        total = cfin[xx].astype(F32) + cfin[4 + xx].astype(F32)
        blocks.append(total + cfin[8 + xx].astype(F32) + cfin[12 + xx].astype(F32))
    full = jnp.concatenate(blocks, axis=0) * scale
    ig_ref[...] = jnp.where(token < live, full.T, 0.0).astype(BF)

    p2_own.wait()

    def p2_wait(j, carry):
        p2_in(j).wait_recv()
        p2(j).wait_send()
        return carry

    lax.fori_loop(1, 32, p2_wait, 0)

    def c_sent(j, carry):
        c_out(j).wait_send()
        return carry

    lax.fori_loop(1, 16, c_sent, 0)

    def p1_sent(j, carry):
        for a in range(3):
            p1(a, j).wait_send()
        return carry

    lax.fori_loop(1, 32, p1_sent, 0)
    for dz in (1, 2, 3):
        u1(dz).wait_send()
    for c in x_sends + w_sends + r_sends:
        c.wait_send()


def shards(old_master, old_moment, old_second, tokens_in, upstream, counts, old_map, new_map):
    slots = jnp.arange(32, dtype=jnp.int32)
    inverse = jnp.sum(jnp.where(old_map[None, :] == slots[:, None], slots[None, :], 0), axis=1)
    hbm = pl.BlockSpec(memory_space=pl.ANY)
    smem = pl.BlockSpec(memory_space=pltpu.SMEM)
    vmem = pl.BlockSpec(memory_space=pltpu.VMEM)
    dma = pltpu.SemaphoreType.DMA
    pieces, input_grad = pl.pallas_call(
        kernel,
        out_shape=(
            jax.ShapeDtypeStruct((3, 2, 4, 32, 1024), BF),
            jax.ShapeDtypeStruct((512, 128), BF),
        ),
        in_specs=[smem] * 3 + [hbm] * 5,
        out_specs=(vmem, vmem),
        scratch_shapes=[
            pltpu.VMEM((3, 128, 2048), F32),
            pltpu.VMEM((512, 4096), BF),
            pltpu.VMEM((3, 2, 4, 32, 1024), BF),
            pltpu.VMEM((32, 2, 32, 128), BF),
            pltpu.VMEM((32, 2, 32, 128), BF),
            pltpu.VMEM((32, 2, 32, 128), BF),
            pltpu.VMEM((512, 2048), BF),
            pltpu.VMEM((4, 256, 512), BF),
            pltpu.VMEM((4, 256, 2048), BF),
            pltpu.VMEM((2, 128, 2048), BF),
            pltpu.VMEM((2, 256, 2048), BF),
            pltpu.VMEM((128, 2048), BF),
            pltpu.VMEM((128, 2048), BF),
            pltpu.VMEM((4, 256, 2048), BF),
            pltpu.VMEM((32, 3, 2, 32, 128), BF),
            pltpu.VMEM((32, 3, 2, 32, 128), BF),
            pltpu.VMEM((8, 2, 2, 32, 512), BF),
            pltpu.VMEM((8, 2, 32, 512), BF),
            pltpu.VMEM((8, 2, 32, 512), BF),
            pltpu.VMEM((16, 32, 512), BF),
            dma((4,)), dma((4,)), dma((4,)), dma((3, 32)), dma((3, 32)), dma((4,)), dma((4,)),
            dma((7,)), dma((7,)), dma((7,)), dma((7,)), dma((32,)), dma((32,)), dma((16,)), dma((16,)),
        ],
        compiler_params=pltpu.CompilerParams(
            collective_id=0, has_side_effects=True, vmem_limit_bytes=56 * 1024 * 1024
        ),
        cost_estimate=pl.CostEstimate(flops=4 * 2**30, bytes_accessed=12 * 2**20, transcendentals=2**18),
    )(
        inverse, new_map, counts,
        old_master.reshape(128, 2048), old_moment.reshape(128, 2048), old_second.reshape(128, 2048),
        tokens_in, upstream,
    )
    pieces = pieces.reshape(3, 1, 1, 256, 1024).astype(F32)
    return pieces[0], pieces[1], pieces[2], input_grad


def solution(mesh):
    pieces = P("tensor", "dp", None, None)
    return jax.shard_map(
        shards,
        mesh=mesh,
        in_specs=(pieces, pieces, pieces, P("dp", None), P("dp", "tensor"), P(), P(), P()),
        out_specs=(pieces, pieces, pieces, P("dp", "tensor")),
        check_vma=False,
    )
```

time: 590 us -> 175 us (0.30)
  waiting for transfers between devices: 408 us -> 0 us
  Pallas kernels: 0 us -> 169 us
  local copies, waits for them, and re-layouts: 69.5 us -> 3.83 us
  starting transfers between devices: 54.8 us -> 0 us
  other arithmetic: 28.7 us -> 1.28 us
  between operations: 16 us -> 0.65 us
  matrix products: 10.7 us -> 0 us
    pallas_call x0 -> x1, Pallas kernels: none -> 169 us  [shards(): pl.pallas_call(kernel, out_shape=(jax.ShapeDtypeStruct((3, 2, 4, 32, 1024...]
    all_to_all x8 -> x0, waiting for transfers between devices: 168 us -> none  [the longest x1 33.1 us: shards(): lax.all_to_all(arrange(recv_moment), 'tensor', split_axis=0, concat_axis=...]
    reduce_scatter x1 -> x0, waiting for transfers between devices: 119 us -> none  [shards(): lax.psum_scatter(spread.reshape(tok_count, width), 'tensor', scatter_dime...]
    psum x1 -> x0, waiting for transfers between devices: 67.3 us -> none  [shards(): lax.psum((lax.dot_general(selected, masked, (((0,), (0,)), ((), ())), pre...]
    all_to_all x8 -> x0, starting transfers between devices: 54.7 us -> none  [the longest x1 12.7 us: shards(): lax.all_to_all(upstream.reshape(lanes, token_slab, atom_cols).astype(jnp....]
    all_gather x1 -> x0, waiting for transfers between devices: 53.2 us -> none  [shards(): lax.all_gather(weights, 'dp', axis=0, tiled=True)]
    mul x6 -> x0, local copies, waits for them, and re-layouts: 20.3 us -> none  [the longest x2 17.5 us: shards(): partial_grad.reshape(tok_count, groups, 1, rows_new)]
    reshape x8 -> x0, local copies, waits for them, and re-layouts: 16.3 us -> none  [the longest x3 8.65 us: arrange(): jnp.take(received, inverse, axis=0).reshape(8, r_new, 2, slab, 2, cols_new)]
  transfers between devices with their start and end apart: 11 -> 0, of which waited for: 10 -> 0; matrix products, arithmetic and copies ran while one was open for 12% -> 0% of each run, Pallas kernels for 0% -> 0%
where the time goes in v1:
time: 175 us
  Pallas kernels  169 us (97%)
  local copies, waits for them, and re-layouts  3.83 us (2%)
    pallas_call x1, Pallas kernels, shards(): pl.pallas_call(kernel, out_shape=(jax.ShapeDtypeStruct((3, 2, 4, 32, 1024...  169 us

profile of v1, /device:TPU:1, one launch (start us, length us, event | category | flops | bytes accessed | tf_op | source)
XLA Modules:
  0.0 174.7 jit_solution(2961368670045910590)
XLA Ops:
  0.6 1.3 select_reduce_fusion.inv_ref
  1.9 168.9 %shard_map.111 = (bf16[3,2,4,32,1024]{4,3,2,1,0:T(8,128)(2,1)}, bf16[512,128]{1,0:T(8,128)(2,1)}) custom-call(s32[32]{0:T(128)} %select_reduce_fusion.inv_ref, s32[32]{0:T(128)} %new_ref.1, s32[8]{0:T(128)} %cnt_ref.1, f32[128,2048]{1,0:T(8,128)} %bitcast.9, f32[128,2048]{1,0:T(8,128)} %bitcast.10, f32[128,2048]{1,0:T(8,128)} %bitcast.11, ...), custom_call_target="tpu_custom_call" | custom-call | flops 4294967296 | bytes 12582912 | tf_op jit(solution)/shard_map/pallas_call | solution.py:413
  170.8 0.0 copy-start
  170.9 3.2 %fusion = (f32[1,2,4,32,1024]{4,3,2,1,0:T(8,128)}, f32[1,2,4,32,1024]{4,3,2,1,0:T(8,128)}, f32[1,2,4,32,1024]{4,3,2,1,0:T(8,128)}) fusion(bf16[3,2,4,32,1024]{4,3,2,1,0:T(8,128)(2,1)} %get-tuple-element.6), kind=kLoop, calls=%fused_computation.2 | loop fusion | bytes 6291456 | tf_op jit(solution)/shard_map/slice | solution.py:455
  174.0 0.0 copy-done
  174.0 0.7 copy.13
Async XLA Ops:
  170.8 3.2 %copy-start = (bf16[512,128]{1,0:T(8,128)(2,1)S(1)}, bf16[512,128]{1,0:T(8,128)(2,1)}, u32[]{:S(2)}) copy-start(bf16[512,128]{1,0:T(8,128)(2,1)} %get-tuple-element.18) | copy-start | bytes 393220

commit v2 on v1

v2 whole, which is shorter than its diff:
```python
import jax
import jax.numpy as jnp
from jax import lax
from jax.experimental import pallas as pl
from jax.experimental.pallas import tpu as pltpu
from jax.sharding import PartitionSpec as P

beta_first = 0.9
beta_second = 0.95
learn_rate = 0.05
decay_rate = 0.1
epsilon = 1e-08

BF = jnp.bfloat16
F32 = jnp.float32
NT = (((1,), (1,)), ((), ()))
NC = 4
PER = NC // 2
RR = 32 // PER
CT = F32


def kernel(
    inv_ref, new_ref, cnt_ref, om_ref, oo_ref, os_ref, tok_ref, up_ref,
    out_ref, ig_ref,
    old, tok, send1, spread_a, spread_b, spread_c, gath, lhs, part, r1, r2, r3, qsend, wg,
    upd, send2, cpart, crecv, csum, cfin,
    ld, us, ur, p1s, p1r, xs, xr, ws, wr, rs, rr, p2s, p2r, ks, kr, cs, cr,
):
    spread = (spread_a, spread_b, spread_c)
    g = lax.axis_index("dp")
    t = lax.axis_index("tensor")
    zl, y = g // 4, g % 4
    z, x, k = t // 8, (t // 2) % 4, t % 2
    zp = 1 - zl
    y_up, y_dn, y_far = (y + 1) % 4, (y + 3) % 4, (y + 2) % 4
    g_up, g_dn, g_pair = zl * 4 + y_up, zl * 4 + y_dn, zp * 4 + y
    x_up, x_dn, x_far = (x + 1) % 4, (x + 3) % 4, (x + 2) % 4
    t_xup, t_xdn = z * 8 + x_up * 2 + k, z * 8 + x_dn * 2 + k
    t_core = z * 8 + x * 2 + 1 - k

    def remote(src, dst, ssem, rsem, dp, tn):
        return pltpu.make_async_remote_copy(
            src_ref=src, dst_ref=dst, send_sem=ssem, recv_sem=rsem,
            device_id=(dp, tn), device_id_type=pl.DeviceIdType.MESH,
        )

    def cols(index, width):
        return pl.ds(pl.multiple_of(index * width, width), width)

    sent = []

    def start(*copies):
        for c in copies:
            c.start()
            sent.append(c)

    loads = [
        pltpu.make_async_copy(src, old.at[a], ld.at[a]) for a, src in enumerate((om_ref, oo_ref, os_ref))
    ] + [pltpu.make_async_copy(tok_ref, tok, ld.at[3])]
    for c in loads:
        c.start()

    barrier = pltpu.get_barrier_semaphore()

    def greet(j, c):
        pl.semaphore_signal(barrier, inc=1, device_id=(g, (t + j) % 32), device_id_type=pl.DeviceIdType.MESH)
        return c

    lax.fori_loop(1, 32, greet, 0)
    for other in (g_up, g_dn, g_pair):
        pl.semaphore_signal(barrier, inc=1, device_id=(other, t), device_id_type=pl.DeviceIdType.MESH)

    def narrow(a):
        loads[a].wait()

        def body(i, c):
            c10, xx = i // 4, i % 4
            send1[a, c10, xx] = old[a, cols(xx, 32), cols(c10, 1024)].astype(BF)
            return c

        lax.fori_loop(0, 8, body, 0)

    def u1(h, dz):
        to = (z + dz) % 4
        return remote(
            up_ref.at[pl.ds(h * 256, 256), cols(to, 128)], gath.at[pl.ds(h * 256, 256), cols(x * 4 + z, 128)],
            us.at[h, dz], ur.at[h, dz], g, to * 8 + x * 2 + k,
        )

    def u1_in(h, dz):
        of = (z + 4 - dz) % 4
        return remote(
            up_ref.at[pl.ds(h * 256, 256), cols(z, 128)], gath.at[pl.ds(h * 256, 256), cols(x * 4 + of, 128)],
            us.at[h, dz], ur.at[h, dz], g, t_core,
        )

    def u1_wait(h):
        if h == 0:
            u1_own.wait()
        for dz in (1, 2, 3):
            u1_in(h, dz).wait_recv()

    u1_own = pltpu.make_async_copy(up_ref.at[:, cols(z, 128)], gath.at[:, cols(x * 4 + z, 128)], ur.at[0, 0])
    def p1(a, j):
        p = (t + j) % 32
        pz, px, pk = p // 8, (p // 2) % 4, p % 2
        return remote(
            send1.at[a, :, px, :, cols(pk * 4 + pz, 128)], spread[a].at[t],
            p1s.at[a, j], p1r.at[a, j], g, p,
        )

    def p1_in(a, j):
        return remote(
            send1.at[a, :, x, :, cols(k * 4 + z, 128)], spread[a].at[(t + 32 - j) % 32],
            p1s.at[a, j], p1r.at[a, j], g, t_core,
        )

    def p1_own(a):
        return pltpu.make_async_copy(send1.at[a, :, x, :, cols(k * 4 + z, 128)], spread[a].at[t], p1r.at[a, 0])

    def p1_start(a):
        p1_own(a).start()

        def body(j, c):
            p1(a, j).start()
            return c

        lax.fori_loop(1, 32, body, 0)

    def p1_wait(a):
        p1_own(a).wait()

        def body(j, c):
            p1_in(a, j).wait_recv()
            return c

        lax.fori_loop(1, 32, body, 0)

    live = cnt_ref[g]
    pick_row = lax.broadcasted_iota(jnp.int32, (128, 512), 0)
    pick_col = lax.broadcasted_iota(jnp.int32, (128, 512), 1)
    chunk_of, so1_of = pick_row // (2 * RR), (pick_row // RR) % 2
    so_of = so1_of * 2 + chunk_of // PER
    r_of = (chunk_of % PER) * RR + pick_row % RR
    pick = jnp.where(pick_col == so_of * 128 + x * 32 + r_of, 1.0, 0.0).astype(BF)
    alive = lax.broadcasted_iota(jnp.int32, (128, 512), 1) < live

    def transpose_tokens(d, c):
        rows = lax.dot_general(pick, tok[:, cols(d, 512)], NT, preferred_element_type=F32)
        rows = jnp.where(alive, rows, 0.0).astype(BF)
        for i in range(NC):
            lhs[i, cols((d % 4) * 2 + d // 4, 2 * RR), :] = rows[i * 2 * RR : (i + 1) * 2 * RR]
        return c

    def ring_x(block, h, way, sem):
        ref = gath.at[pl.ds(h * 256, 256), cols(block, 512)]
        return remote(ref, ref, xs.at[sem], xr.at[sem], g, way)

    def place(q):
        zs, half = q % 4, q // 4
        return zs * 2 + half // 2, half % 2

    def weights(q, c):
        bo, c10 = place(q)
        for so in range(4):
            wg[y, pl.ds(pl.multiple_of(zl * 128 + so * 32, 32), 32), cols(q, 128)] = spread[0][inv_ref[bo * 4 + so], c10]
        return c

    def ring_w(yy, zz, to, sem):
        ref = wg.at[yy, cols(zz, 128), :]
        return remote(ref, ref, ws.at[sem], wr.at[sem], to, t)

    def block(ref, i, yy, zz):
        return ref.at[i, cols(yy * 2 + zz, 2 * RR), :]

    def partial(i):
        def body(c, carry):
            part[i, :, cols(c, 512)] = jnp.dot(
                lhs[i], gath[:, cols(c, 512)], preferred_element_type=F32
            ).astype(BF)
            return carry

        lax.fori_loop(0, 4, body, 0)

    def sum_copy(i, n, src, dst, to):
        return remote(src, dst, rs.at[i, n], rr.at[i, n], to, t)

    def far_up(i):
        return sum_copy(i, 0, block(part, i, y_far, 0), r1.at[i, 0], g_up)

    def far_dn(i):
        return sum_copy(i, 1, block(part, i, y_far, 1), r1.at[i, 1], g_dn)

    def near_up(i, zz):
        return sum_copy(i, 2 + zz, block(part, i, y_up, zz), r2.at[i, 0, zz], g_up)

    def near_dn(i, zz):
        return sum_copy(i, 4 + zz, block(part, i, y_dn, zz), r2.at[i, 1, zz], g_dn)

    def pair_copy(i):
        return sum_copy(i, 6, qsend.at[i], r3.at[i], g_pair)

    def add_into(i, yy, zz, side):
        def body(c, carry):
            at = (i, cols(yy * 2 + zz, 2 * RR), cols(c, 512))
            part[at] = (part[at].astype(F32) + r1[i, side, :, cols(c, 512)].astype(F32)).astype(BF)
            return carry

        lax.fori_loop(0, 4, body, 0)

    def sum_first(i):
        start(far_up(i), far_dn(i), near_up(i, 1), near_dn(i, 0))

    def sum_second(i):
        far_up(i).wait_recv()
        add_into(i, y_up, 0, 0)
        start(near_up(i, 0))
        far_dn(i).wait_recv()
        add_into(i, y_dn, 1, 1)
        start(near_dn(i, 1))

    def sum_third(i):
        for zz in range(2):
            near_up(i, zz).wait_recv()
            near_dn(i, zz).wait_recv()

        def body(c, carry):
            here = cols(c, 512)
            total = part[i, cols(y * 2 + zp, 2 * RR), here].astype(F32) + r2[i, 0, zp, :, here].astype(F32)
            qsend[i, :, here] = (total + r2[i, 1, zp, :, here].astype(F32)).astype(BF)
            return carry

        lax.fori_loop(0, 4, body, 0)
        start(pair_copy(i))

    fix_first = 1.0 - beta_first**10
    fix_second = 1.0 - beta_second**10
    scale = 1.0 / 64.0

    def adamw(i):
        pair_copy(i).wait_recv()
        so0, r0 = i // PER, (i % PER) * RR

        def body(q, carry):
            bo, c10 = place(q)
            here = cols(q, 128)
            for so1 in range(2):
                slot = inv_ref[bo * 4 + so1 * 2 + so0]
                at = slice(so1 * RR, (so1 + 1) * RR)
                mine = pl.ds(pl.multiple_of((y * 2 + zl) * 2 * RR + so1 * RR, RR), RR)
                grad = part[i, mine, here].astype(F32) + r2[i, 0, zl, at, here].astype(F32)
                grad = grad + r2[i, 1, zl, at, here].astype(F32) + r3[i, at, here].astype(F32)
                grad = grad * scale
                rows = slice(r0, r0 + RR)
                master = spread[0][slot, c10, rows].astype(F32)
                moment = beta_first * spread[1][slot, c10, rows].astype(F32) + (1.0 - beta_first) * grad
                second = beta_second * spread[2][slot, c10, rows].astype(F32) + (1.0 - beta_second) * grad * grad
                update = moment / fix_first / (jnp.sqrt(second / fix_second) + epsilon) + decay_rate * master
                piece = (bo * 2 + c10) * 2 + so1
                upd[i, piece, 0] = (master - learn_rate * update).astype(BF)
                upd[i, piece, 1] = moment.astype(BF)
                upd[i, piece, 2] = second.astype(BF)
            return carry

        lax.fori_loop(0, 16, body, 0)

    def p2_place(i, px, pk, pz):
        return out_ref.at[:, i // PER, px, pl.ds((i % PER) * RR, RR), cols(pk * 4 + pz, 128)]

    def p2(i, j):
        p = (t + j) % 32
        return remote(send2[i].at[p], p2_place(i, x, k, z), p2s.at[i, j], p2r.at[i, j], g, p)

    def p2_in(i, j):
        p = (t + 32 - j) % 32
        return remote(
            send2[i].at[t], p2_place(i, (p // 2) % 4, p % 2, p // 8), p2s.at[i, j], p2r.at[i, j], g, t_core
        )

    def p2_own(i):
        return pltpu.make_async_copy(send2[i].at[t], p2_place(i, x, k, z), p2r.at[i, 0])

    def p2_start(i):
        def body(j, carry):
            p = (t + j) % 32
            send2[i][p] = upd[i, new_ref[p]]
            p2(i, j).start()
            return carry

        lax.fori_loop(1, 32, body, 0)
        send2[i][t] = upd[i, new_ref[t]]
        p2_own(i).start()

    def back(yy):
        rows = lax.dot_general(wg[yy], gath[...], NT, preferred_element_type=F32)
        for zz in range(2):
            for so in range(4):
                at = zz * 128 + so * 32
                cpart[zz * 4 + yy, so // 2, so % 2] = rows[at : at + 32].astype(CT)

    def core_copy(i, yy, zz):
        return remote(
            cpart.at[zz * 4 + yy, :, 1 - k], crecv.at[zz * 4 + yy], ks.at[i, zz], kr.at[i, zz], g, t_core
        )

    def back_send(i, yy):
        back(yy)
        start(core_copy(i, yy, 0), core_copy(i, yy, 1))

    me16 = z * 4 + x

    def c_out(p):
        j = (p - me16 + 16) % 16
        return remote(csum.at[p // 2, p % 2], cfin.at[me16], cs.at[j], cr.at[j], g, p * 2 + k)

    c_own = pltpu.make_async_copy(csum.at[me16 // 2, me16 % 2], cfin.at[me16], cr.at[0])

    def back_sum(i, yy):
        for zz in range(2):
            d = zz * 4 + yy
            core_copy(i, yy, zz).wait_recv()
            csum[d] = (cpart[d, :, k].astype(F32) + crecv[d].astype(F32)).astype(BF)
            for so1 in range(2):
                p = d * 2 + so1

                @pl.when(p != me16)
                def _():
                    c_out(p).start()

                @pl.when(p == me16)
                def _():
                    c_own.start()

    pl.semaphore_wait(barrier, 34)
    u1_own.start()
    narrow(0)
    p1_start(0)
    loads[3].wait()
    lax.fori_loop(0, 8, transpose_tokens, 0)
    for h in range(2):
        for dz in (2, 1, 3):
            start(u1(h, dz))
    narrow(1)
    narrow(2)
    p1_wait(0)
    lax.fori_loop(0, 16, weights, 0)
    start(ring_w(y, zl, g_pair, 2), ring_w(y, zl, g_up, 0), ring_w(y, zl, g_dn, 1))
    u1_wait(0)
    start(ring_x(x, 0, t_xup, 0))
    u1_wait(1)
    start(ring_x(x, 1, t_xdn, 1), ring_x(x, 1, t_xup, 2), ring_x(x, 0, t_xdn, 3))
    p1_start(1)
    p1_start(2)
    ring_w(y_dn, zl, g_up, 0).wait_recv()
    start(ring_w(y_dn, zl, g_up, 5))
    ring_w(y_up, zl, g_dn, 1).wait_recv()
    ring_w(y, zp, g_pair, 2).wait_recv()
    start(ring_w(y, zp, g_up, 3), ring_w(y, zp, g_dn, 4))
    ring_x(x_dn, 0, t_xup, 0).wait_recv()
    start(ring_x(x_dn, 0, t_xup, 4))
    ring_x(x_up, 1, t_xdn, 1).wait_recv()
    start(ring_x(x_up, 1, t_xdn, 5))
    ring_x(x_dn, 1, t_xup, 2).wait_recv()
    ring_x(x_up, 0, t_xdn, 3).wait_recv()
    ring_x(x_far, 0, t_xup, 4).wait_recv()
    ring_x(x_far, 1, t_xdn, 5).wait_recv()
    partial(0)
    sum_first(0)
    ring_w(y_up, zp, g_dn, 4).wait_recv()
    start(ring_w(y_up, zp, g_dn, 6))
    back_send(0, y)
    partial(1)
    sum_first(1)
    sum_second(0)
    partial(2)
    sum_first(2)
    ring_w(y_dn, zp, g_up, 3).wait_recv()
    back_send(1, y_dn)
    back_send(2, y_up)
    back_sum(0, y)
    sum_second(1)
    sum_third(0)
    back_sum(1, y_dn)
    back_sum(2, y_up)
    partial(3)
    sum_first(3)
    ring_w(y_far, zl, g_up, 5).wait_recv()
    ring_w(y_far, zp, g_dn, 6).wait_recv()
    back_send(3, y_far)
    sum_second(2)
    sum_third(1)
    p1_wait(1)
    p1_wait(2)
    back_sum(3, y_far)
    adamw(0)
    p2_start(0)
    sum_second(3)
    sum_third(2)
    adamw(1)
    p2_start(1)
    sum_third(3)
    adamw(2)
    p2_start(2)
    adamw(3)
    p2_start(3)

    c_own.wait()

    def c_wait(j, carry):
        remote(csum.at[0, 0], cfin.at[(me16 + 16 - j) % 16], cs.at[j], cr.at[j], g, t_core).wait_recv()
        return carry

    lax.fori_loop(1, 16, c_wait, 0)
    token = lax.broadcasted_iota(jnp.int32, (512, 128), 0)
    blocks = []
    for xx in range(4):
        total = cfin[xx].astype(F32) + cfin[4 + xx].astype(F32)
        blocks.append(total + cfin[8 + xx].astype(F32) + cfin[12 + xx].astype(F32))
    full = jnp.concatenate(blocks, axis=0) * scale
    ig_ref[...] = jnp.where(token < live, full.T, 0.0).astype(BF)

    for i in range(NC):
        p2_own(i).wait()

        def p2_wait(j, carry):
            p2_in(i, j).wait_recv()
            p2(i, j).wait_send()
            return carry

        lax.fori_loop(1, 32, p2_wait, 0)

    def c_sent(j, carry):
        c_out((me16 + j) % 16).wait_send()
        return carry

    lax.fori_loop(1, 16, c_sent, 0)

    def p1_sent(j, carry):
        for a in range(3):
            p1(a, j).wait_send()
        return carry

    lax.fori_loop(1, 32, p1_sent, 0)
    for c in sent:
        c.wait_send()


def shards(old_master, old_moment, old_second, tokens_in, upstream, counts, old_map, new_map):
    slots = jnp.arange(32, dtype=jnp.int32)
    inverse = jnp.sum(jnp.where(old_map[None, :] == slots[:, None], slots[None, :], 0), axis=1)
    hbm = pl.BlockSpec(memory_space=pl.ANY)
    smem = pl.BlockSpec(memory_space=pltpu.SMEM)
    vmem = pl.BlockSpec(memory_space=pltpu.VMEM)
    dma = pltpu.SemaphoreType.DMA
    pieces, input_grad = pl.pallas_call(
        kernel,
        out_shape=(
            jax.ShapeDtypeStruct((3, 2, 4, 32, 1024), BF),
            jax.ShapeDtypeStruct((512, 128), BF),
        ),
        in_specs=[smem] * 3 + [hbm] * 5,
        out_specs=(vmem, vmem),
        scratch_shapes=[
            pltpu.VMEM((3, 128, 2048), F32),
            pltpu.VMEM((512, 4096), BF),
            pltpu.VMEM((3, 2, 4, 32, 1024), BF),
            pltpu.VMEM((32, 2, 32, 128), BF),
            pltpu.VMEM((32, 2, 32, 128), BF),
            pltpu.VMEM((32, 2, 32, 128), BF),
            pltpu.VMEM((512, 2048), BF),
            pltpu.VMEM((NC, 16 * RR, 512), BF),
            pltpu.VMEM((NC, 16 * RR, 2048), BF),
            pltpu.VMEM((NC, 2, 2 * RR, 2048), BF),
            pltpu.VMEM((NC, 2, 2, 2 * RR, 2048), BF),
            pltpu.VMEM((NC, 2 * RR, 2048), BF),
            pltpu.VMEM((NC, 2 * RR, 2048), BF),
            pltpu.VMEM((4, 256, 2048), BF),
            pltpu.VMEM((NC, 32, 3, RR, 128), BF),
            [pltpu.VMEM((32, 3, RR, 128), BF)] * NC,
            pltpu.VMEM((8, 2, 2, 32, 512), CT),
            pltpu.VMEM((8, 2, 32, 512), CT),
            pltpu.VMEM((8, 2, 32, 512), BF),
            pltpu.VMEM((16, 32, 512), BF),
            dma((4,)), dma((2, 4)), dma((2, 4)), dma((3, 32)), dma((3, 32)), dma((6,)), dma((6,)),
            dma((7,)), dma((7,)), dma((NC, 7)), dma((NC, 7)), dma((NC, 32)), dma((NC, 32)),
            dma((4, 2)), dma((4, 2)), dma((16,)), dma((16,)),
        ],
        compiler_params=pltpu.CompilerParams(
            collective_id=0, has_side_effects=True, vmem_limit_bytes=56 * 1024 * 1024
        ),
        cost_estimate=pl.CostEstimate(flops=4 * 2**30, bytes_accessed=12 * 2**20, transcendentals=2**18),
    )(
        inverse, new_map, counts,
        old_master.reshape(128, 2048), old_moment.reshape(128, 2048), old_second.reshape(128, 2048),
        tokens_in, upstream,
    )
    pieces = pieces.reshape(3, 1, 1, 256, 1024).astype(F32)
    return pieces[0], pieces[1], pieces[2], input_grad


def solution(mesh):
    pieces = P("tensor", "dp", None, None)
    return jax.shard_map(
        shards,
        mesh=mesh,
        in_specs=(pieces, pieces, pieces, P("dp", None), P("dp", "tensor"), P(), P(), P()),
        out_specs=(pieces, pieces, pieces, P("dp", "tensor")),
        check_vma=False,
    )
```

time: 175 us -> 160 us (0.914)
  Pallas kernels: 169 us -> 154 us
    pallas_call x1, Pallas kernels: 169 us -> 154 us  [shards(): pl.pallas_call(kernel, out_shape=(jax.ShapeDtypeStruct((3, 2, 4, 32, 1024...]
where the time goes in v2:
time: 160 us
  Pallas kernels  154 us (96%)
  local copies, waits for them, and re-layouts  3.83 us (2%)
    pallas_call x1, Pallas kernels, shards(): pl.pallas_call(kernel, out_shape=(jax.ShapeDtypeStruct((3, 2, 4, 32, 1024...  154 us

profile of v2, /device:TPU:1, one launch (start us, length us, event | category | flops | bytes accessed | tf_op | source)
XLA Modules:
  0.0 159.7 jit_solution(1548322121061391552)
XLA Ops:
  0.6 1.3 select_reduce_fusion.inv_ref
  1.9 154.0 %shard_map.111 = (bf16[3,2,4,32,1024]{4,3,2,1,0:T(8,128)(2,1)}, bf16[512,128]{1,0:T(8,128)(2,1)}) custom-call(s32[32]{0:T(128)} %select_reduce_fusion.inv_ref, s32[32]{0:T(128)} %new_ref.1, s32[8]{0:T(128)} %cnt_ref.1, f32[128,2048]{1,0:T(8,128)} %bitcast.9, f32[128,2048]{1,0:T(8,128)} %bitcast.10, f32[128,2048]{1,0:T(8,128)} %bitcast.11, ...), custom_call_target="tpu_custom_call" | custom-call | flops 4294967296 | bytes 12582912 | tf_op jit(solution)/shard_map/pallas_call | solution.py:456
  155.9 0.0 copy-start
  155.9 3.2 %fusion = (f32[1,2,4,32,1024]{4,3,2,1,0:T(8,128)}, f32[1,2,4,32,1024]{4,3,2,1,0:T(8,128)}, f32[1,2,4,32,1024]{4,3,2,1,0:T(8,128)}) fusion(bf16[3,2,4,32,1024]{4,3,2,1,0:T(8,128)(2,1)} %get-tuple-element.6), kind=kLoop, calls=%fused_computation.2 | loop fusion | bytes 6291456 | tf_op jit(solution)/shard_map/slice | solution.py:499
  159.1 0.0 copy-done
  159.1 0.7 copy.13
Async XLA Ops:
  155.9 3.2 %copy-start = (bf16[512,128]{1,0:T(8,128)(2,1)S(1)}, bf16[512,128]{1,0:T(8,128)(2,1)}, u32[]{:S(2)}) copy-start(bf16[512,128]{1,0:T(8,128)(2,1)} %get-tuple-element.18) | copy-start | bytes 393220

commit v3 on v2

v3 whole, which is shorter than its diff:
```python
import jax
import jax.numpy as jnp
from jax import lax
from jax.experimental import pallas as pl
from jax.experimental.pallas import tpu as pltpu
from jax.sharding import PartitionSpec as P

beta_first = 0.9
beta_second = 0.95
learn_rate = 0.05
decay_rate = 0.1
epsilon = 1e-08

BF = jnp.bfloat16
F32 = jnp.float32
NT = (((1,), (1,)), ((), ()))
NC = 4
PER = NC // 2
RR = 32 // PER
CT = F32


def kernel(
    inv_ref, new_ref, cnt_ref, om_ref, oo_ref, os_ref, tok_ref, up_ref,
    out_ref, ig_ref,
    old, tok, send1, spread_a, spread_b, spread_c, gath, lhs, tsend, acc, part, r1, r2, wg,
    upd, send2, cpart, crecv, csum, cfin,
    ld, us, ur, es, er, ts, tr, p1s, p1r, xs, xr, ws, wr, rs, rr, p2s, p2r, ks, kr, cs, cr,
):
    spread = (spread_a, spread_b, spread_c)
    g = lax.axis_index("dp")
    t = lax.axis_index("tensor")
    zl, y = g // 4, g % 4
    z, x, k = t // 8, (t // 2) % 4, t % 2
    zp = 1 - zl
    y_up, y_dn, y_far = (y + 1) % 4, (y + 3) % 4, (y + 2) % 4
    g_up, g_dn, g_pair = zl * 4 + y_up, zl * 4 + y_dn, zp * 4 + y
    x_up, x_dn, x_far = (x + 1) % 4, (x + 3) % 4, (x + 2) % 4
    t_xup, t_xdn = z * 8 + x_up * 2 + k, z * 8 + x_dn * 2 + k
    t_core = z * 8 + x * 2 + 1 - k

    def remote(src, dst, ssem, rsem, dp, tn):
        return pltpu.make_async_remote_copy(
            src_ref=src, dst_ref=dst, send_sem=ssem, recv_sem=rsem,
            device_id=(dp, tn), device_id_type=pl.DeviceIdType.MESH,
        )

    def cols(index, width):
        return pl.ds(pl.multiple_of(index * width, width), width)

    sent = []

    def start(*copies):
        for c in copies:
            c.start()
            sent.append(c)

    loads = [
        pltpu.make_async_copy(src, old.at[a], ld.at[a]) for a, src in enumerate((om_ref, oo_ref, os_ref))
    ] + [pltpu.make_async_copy(tok_ref, tok, ld.at[3])]
    for c in loads:
        c.start()

    barrier = pltpu.get_barrier_semaphore()

    def greet(j, c):
        pl.semaphore_signal(barrier, inc=1, device_id=(g, (t + j) % 32), device_id_type=pl.DeviceIdType.MESH)
        return c

    lax.fori_loop(1, 32, greet, 0)
    for other in (g_up, g_dn):
        pl.semaphore_signal(barrier, inc=1, device_id=(other, t), device_id_type=pl.DeviceIdType.MESH)

    def greet_pair(j, c):
        pl.semaphore_signal(barrier, inc=1, device_id=(g_pair, j * 2 + k), device_id_type=pl.DeviceIdType.MESH)
        return c

    lax.fori_loop(0, 16, greet_pair, 0)

    def narrow(a):
        loads[a].wait()

        def body(i, c):
            c10, xx = i // 4, i % 4
            send1[a, c10, xx] = old[a, cols(xx, 32), cols(c10, 1024)].astype(BF)
            return c

        lax.fori_loop(0, 8, body, 0)

    def half(zz, h):
        return pl.ds(pl.multiple_of(zz * 512 + h * 256, 256), 256)

    def u1(h, dz):
        to = (z + dz) % 4
        return remote(
            up_ref.at[pl.ds(h * 256, 256), cols(to, 128)], gath.at[half(zl, h), cols(x * 4 + z, 128)],
            us.at[h, dz], ur.at[h, dz], g, to * 8 + x * 2 + k,
        )

    def u1_in(h, dz):
        of = (z + 4 - dz) % 4
        return remote(
            up_ref.at[pl.ds(h * 256, 256), cols(z, 128)], gath.at[half(zl, h), cols(x * 4 + of, 128)],
            us.at[h, dz], ur.at[h, dz], g, t_core,
        )

    def u1_wait(h):
        if h == 0:
            u1_own.wait()
        for dz in (1, 2, 3):
            u1_in(h, dz).wait_recv()

    u1_own = pltpu.make_async_copy(up_ref.at[:, cols(z, 128)], gath.at[cols(zl, 512), cols(x * 4 + z, 128)], ur.at[0, 0])

    def u2(zz, h):
        ref = gath.at[half(zz, h), cols(x, 512)]
        return remote(ref, ref, es.at[h], er.at[h], g_pair, t)

    def p1(a, j):
        p = (t + j) % 32
        pz, px, pk = p // 8, (p // 2) % 4, p % 2
        return remote(
            send1.at[a, :, px, :, cols(pk * 4 + pz, 128)], spread[a].at[t],
            p1s.at[a, j], p1r.at[a, j], g, p,
        )

    def p1_in(a, j):
        return remote(
            send1.at[a, :, x, :, cols(k * 4 + z, 128)], spread[a].at[(t + 32 - j) % 32],
            p1s.at[a, j], p1r.at[a, j], g, t_core,
        )

    def p1_own(a):
        return pltpu.make_async_copy(send1.at[a, :, x, :, cols(k * 4 + z, 128)], spread[a].at[t], p1r.at[a, 0])

    def p1_start(a):
        p1_own(a).start()

        def body(j, c):
            p1(a, j).start()
            return c

        lax.fori_loop(1, 32, body, 0)

    def p1_wait(a):
        p1_own(a).wait()

        def body(j, c):
            p1_in(a, j).wait_recv()
            return c

        lax.fori_loop(1, 32, body, 0)

    live = cnt_ref[g]
    pick_row = lax.broadcasted_iota(jnp.int32, (128, 512), 0)
    pick_col = lax.broadcasted_iota(jnp.int32, (128, 512), 1)
    chunk_of, so1_of = pick_row // (2 * RR), (pick_row // RR) % 2
    so_of = so1_of * 2 + chunk_of // PER
    r_of = (chunk_of % PER) * RR + pick_row % RR
    pick = jnp.where(pick_col == so_of * 128 + x * 32 + r_of, 1.0, 0.0).astype(BF)
    alive = lax.broadcasted_iota(jnp.int32, (128, 512), 1) < live

    def transpose_tokens(yy, c):
        for zz, ref, where in ((zl, lhs, cols(zl, 512)), (zp, tsend, pl.ds(0, 512))):
            rows = lax.dot_general(pick, tok[:, cols(zz * 4 + yy, 512)], NT, preferred_element_type=F32)
            rows = jnp.where(alive, rows, 0.0).astype(BF)
            for i in range(NC):
                ref[cols(i * 4 + yy, 2 * RR), where] = rows[i * 2 * RR : (i + 1) * 2 * RR]
        return c

    def tokens_pair(zz, kk):
        rows = cols(kk, 256)
        return remote(tsend.at[rows], lhs.at[rows, cols(zz, 512)], ts.at[0], tr.at[0], g_pair, t)

    def tokens_core(kk):
        ref = lhs.at[cols(kk, 256), cols(zp, 512)]
        return remote(ref, ref, ts.at[1], tr.at[1], g, t_core)

    def ring_x(zz, block, h, way, sem):
        ref = gath.at[half(zz, h), cols(block, 512)]
        at = sem if zz is zl else 6 + sem
        return remote(ref, ref, xs.at[at], xr.at[at], g, way)

    def place(q):
        zs, half = q % 4, q // 4
        return zs * 2 + half // 2, half % 2

    def weights(q, c):
        bo, c10 = place(q)
        for so in range(4):
            wg[cols(y * 4 + so, 32), cols(q, 128)] = spread[0][inv_ref[bo * 4 + so], c10]
        return c

    def ring_w(yy, start_row, rows, to, sem):
        ref = wg.at[pl.ds(pl.multiple_of(yy * 128 + start_row, 64), rows), :]
        return remote(ref, ref, ws.at[sem], wr.at[sem], to, t)

    def block(i, yy, so1):
        return part.at[cols(i * 8 + yy * 2 + so1, RR), :]

    def partial(zz):
        def body(c, carry):
            here = cols(c, 512)
            product = jnp.dot(
                lhs[:, cols(zz, 512)], gath[cols(zz, 512), here], preferred_element_type=F32
            )
            if zz is zl:
                acc[:, here] = product
            else:
                part[:, here] = (acc[:, here] + product).astype(BF)
            return carry

        lax.fori_loop(0, 4, body, 0)

    def sum_copy(i, n, src, dst, to):
        return remote(src, dst, rs.at[i, n], rr.at[i, n], to, t)

    def far_up(i):
        return sum_copy(i, 0, block(i, y_far, 0), r1.at[i, 0], g_up)

    def far_dn(i):
        return sum_copy(i, 1, block(i, y_far, 1), r1.at[i, 1], g_dn)

    def near_up(i, so1):
        return sum_copy(i, 2 + so1, block(i, y_up, so1), r2.at[i, 0, so1], g_up)

    def near_dn(i, so1):
        return sum_copy(i, 4 + so1, block(i, y_dn, so1), r2.at[i, 1, so1], g_dn)

    def add_into(i, yy, so1):
        def body(c, carry):
            at = (cols(i * 8 + yy * 2 + so1, RR), cols(c, 512))
            part[at] = (part[at].astype(F32) + r1[i, so1, :, cols(c, 512)].astype(F32)).astype(BF)
            return carry

        lax.fori_loop(0, 4, body, 0)

    def sum_first(i):
        start(far_up(i), far_dn(i), near_up(i, 1), near_dn(i, 0))

    def sum_second(i):
        far_up(i).wait_recv()
        add_into(i, y_up, 0)
        start(near_up(i, 0))
        far_dn(i).wait_recv()
        add_into(i, y_dn, 1)
        start(near_dn(i, 1))

    fix_first = 1.0 - beta_first**10
    fix_second = 1.0 - beta_second**10
    scale = 1.0 / 64.0

    def adamw(i):
        for so1 in range(2):
            near_up(i, so1).wait_recv()
            near_dn(i, so1).wait_recv()
        so0, r0 = i // PER, (i % PER) * RR

        def body(q, carry):
            bo, c10 = place(q)
            here = cols(q, 128)
            for so1 in range(2):
                slot = inv_ref[bo * 4 + so1 * 2 + so0]
                mine = cols(i * 8 + y * 2 + so1, RR)
                grad = part[mine, here].astype(F32) + r2[i, 0, so1, :, here].astype(F32)
                grad = grad + r2[i, 1, so1, :, here].astype(F32)
                grad = grad * scale
                rows = slice(r0, r0 + RR)
                master = spread[0][slot, c10, rows].astype(F32)
                moment = beta_first * spread[1][slot, c10, rows].astype(F32) + (1.0 - beta_first) * grad
                second = beta_second * spread[2][slot, c10, rows].astype(F32) + (1.0 - beta_second) * grad * grad
                update = moment / fix_first / (jnp.sqrt(second / fix_second) + epsilon) + decay_rate * master
                piece = (bo * 2 + c10) * 2 + so1
                upd[i, piece, 0] = (master - learn_rate * update).astype(BF)
                upd[i, piece, 1] = moment.astype(BF)
                upd[i, piece, 2] = second.astype(BF)
            return carry

        lax.fori_loop(0, 16, body, 0)

    def p2_place(i, px, pk, pz):
        return out_ref.at[:, i // PER, px, pl.ds((i % PER) * RR, RR), cols(pk * 4 + pz, 128)]

    def p2(i, j):
        p = (t + j) % 32
        return remote(send2[i].at[p], p2_place(i, x, k, z), p2s.at[i, j], p2r.at[i, j], g, p)

    def p2_in(i, j):
        p = (t + 32 - j) % 32
        return remote(
            send2[i].at[t], p2_place(i, (p // 2) % 4, p % 2, p // 8), p2s.at[i, j], p2r.at[i, j], g, t_core
        )

    def p2_own(i):
        return pltpu.make_async_copy(send2[i].at[t], p2_place(i, x, k, z), p2r.at[i, 0])

    def p2_start(i):
        def body(j, carry):
            p = (t + j) % 32
            send2[i][p] = upd[i, new_ref[p]]
            p2(i, j).start()
            return carry

        lax.fori_loop(1, 32, body, 0)
        send2[i][t] = upd[i, new_ref[t]]
        p2_own(i).start()

    def back(tz):
        def body(c, carry):
            rows = lax.dot_general(
                wg[...], gath[cols(tz * 2 + c, 256), :], NT, preferred_element_type=F32
            )
            for yy in range(4):
                for so in range(4):
                    at = yy * 128 + so * 32
                    cpart[tz, yy, so // 2, so % 2, :, cols(c, 256)] = rows[at : at + 32].astype(CT)
            return carry

        lax.fori_loop(0, 2, body, 0)

    def core_copy(tz):
        at = 0 if tz is zl else 1
        return remote(cpart.at[tz, :, :, 1 - k], crecv.at[tz], ks.at[at], kr.at[at], g, t_core)

    def back_send(tz):
        back(tz)
        start(core_copy(tz))

    me16 = z * 4 + x
    c_own = pltpu.make_async_copy(csum.at[zl, (z % 2) * 2 + x // 2, x % 2], cfin.at[me16], cr.at[me16])

    def c_parts(tz):
        for yy in range(4):
            for so1 in range(2):
                pz, px = zl * 2 + yy // 2, (yy % 2) * 2 + so1
                here = jnp.logical_and(pz == z, px == x)
                copy = remote(
                    csum.at[tz, yy, so1], cfin.at[me16], cs.at[0 if tz is zl else 1, yy, so1], cr.at[me16],
                    tz * 4 + y, pz * 8 + px * 2 + k,
                )
                yield here, copy

    def back_sum(tz):
        core_copy(tz).wait_recv()

        def body(yy, carry):
            csum[tz, yy] = (cpart[tz, yy, :, k].astype(F32) + crecv[tz, yy].astype(F32)).astype(BF)
            return carry

        lax.fori_loop(0, 4, body, 0)
        for here, copy in c_parts(tz):
            if tz is zl:

                @pl.when(jnp.logical_not(here))
                def _():
                    copy.start()

                @pl.when(here)
                def _():
                    c_own.start()

            else:
                start(copy)

    narrow(0)
    pl.semaphore_wait(barrier, 49)
    u1_own.start()
    for h in range(2):
        for dz in (2, 1, 3):
            start(u1(h, dz))
    loads[3].wait()
    lax.fori_loop(0, 4, transpose_tokens, 0)
    narrow(1)
    narrow(2)
    u1_wait(0)
    start(ring_x(zl, x, 0, t_xup, 0), u2(zl, 0))
    p1_start(0)
    u1_wait(1)
    start(ring_x(zl, x, 1, t_xdn, 1), u2(zl, 1), ring_x(zl, x, 1, t_xup, 2), ring_x(zl, x, 0, t_xdn, 3))
    start(tokens_pair(zl, k))
    ring_x(zl, x_dn, 0, t_xup, 0).wait_recv()
    start(ring_x(zl, x_dn, 0, t_xup, 4))
    ring_x(zl, x_up, 1, t_xdn, 1).wait_recv()
    start(ring_x(zl, x_up, 1, t_xdn, 5))
    u2(zp, 0).wait_recv()
    start(ring_x(zp, x, 0, t_xup, 0))
    u2(zp, 1).wait_recv()
    start(ring_x(zp, x, 1, t_xdn, 1), ring_x(zp, x, 1, t_xup, 2), ring_x(zp, x, 0, t_xdn, 3))
    p1_start(1)
    p1_wait(0)
    lax.fori_loop(0, 16, weights, 0)
    start(ring_w(y, 0, 128, g_up, 0), ring_w(y, 0, 128, g_dn, 1))
    p1_start(2)
    tokens_pair(zp, k).wait_recv()
    start(tokens_core(k))
    ring_x(zp, x_dn, 0, t_xup, 0).wait_recv()
    start(ring_x(zp, x_dn, 0, t_xup, 4))
    ring_x(zp, x_up, 1, t_xdn, 1).wait_recv()
    start(ring_x(zp, x_up, 1, t_xdn, 5))
    ring_w(y_dn, 0, 128, g_up, 0).wait_recv()
    start(ring_w(y_dn, 0, 64, g_up, 2))
    ring_w(y_up, 0, 128, g_dn, 1).wait_recv()
    start(ring_w(y_up, 64, 64, g_dn, 3))
    ring_x(zl, x_dn, 1, t_xup, 2).wait_recv()
    ring_x(zl, x_up, 0, t_xdn, 3).wait_recv()
    ring_x(zl, x_far, 0, t_xup, 4).wait_recv()
    ring_x(zl, x_far, 1, t_xdn, 5).wait_recv()
    partial(zl)
    ring_w(y_far, 0, 64, g_up, 2).wait_recv()
    ring_w(y_far, 64, 64, g_dn, 3).wait_recv()
    back_send(zl)
    back_sum(zl)
    ring_x(zp, x_dn, 1, t_xup, 2).wait_recv()
    ring_x(zp, x_up, 0, t_xdn, 3).wait_recv()
    ring_x(zp, x_far, 0, t_xup, 4).wait_recv()
    ring_x(zp, x_far, 1, t_xdn, 5).wait_recv()
    tokens_core(1 - k).wait_recv()
    partial(zp)
    sum_first(0)
    sum_first(1)
    back_send(zp)
    sum_second(0)
    sum_first(2)
    sum_second(1)
    sum_first(3)
    p1_wait(1)
    p1_wait(2)
    adamw(0)
    p2_start(0)
    back_sum(zp)
    sum_second(2)
    adamw(1)
    p2_start(1)
    sum_second(3)
    adamw(2)
    p2_start(2)
    adamw(3)
    p2_start(3)

    def c_wait(j, carry):
        remote(csum.at[0, 0, 0], cfin.at[j], cs.at[0, 0, 0], cr.at[j], g, t_core).wait_recv()
        return carry

    lax.fori_loop(0, 16, c_wait, 0)
    token = lax.broadcasted_iota(jnp.int32, (512, 128), 0)
    blocks = []
    for xx in range(4):
        total = cfin[xx].astype(F32) + cfin[4 + xx].astype(F32)
        blocks.append(total + cfin[8 + xx].astype(F32) + cfin[12 + xx].astype(F32))
    full = jnp.concatenate(blocks, axis=0) * scale
    ig_ref[...] = jnp.where(token < live, full.T, 0.0).astype(BF)

    for i in range(NC):
        p2_own(i).wait()

        def p2_wait(j, carry):
            p2_in(i, j).wait_recv()
            p2(i, j).wait_send()
            return carry

        lax.fori_loop(1, 32, p2_wait, 0)

    for here, copy in c_parts(zl):

        @pl.when(jnp.logical_not(here))
        def _():
            copy.wait_send()


    def p1_sent(j, carry):
        for a in range(3):
            p1(a, j).wait_send()
        return carry

    lax.fori_loop(1, 32, p1_sent, 0)
    for c in sent:
        c.wait_send()


def shards(old_master, old_moment, old_second, tokens_in, upstream, counts, old_map, new_map):
    slots = jnp.arange(32, dtype=jnp.int32)
    inverse = jnp.sum(jnp.where(old_map[None, :] == slots[:, None], slots[None, :], 0), axis=1)
    hbm = pl.BlockSpec(memory_space=pl.ANY)
    smem = pl.BlockSpec(memory_space=pltpu.SMEM)
    vmem = pl.BlockSpec(memory_space=pltpu.VMEM)
    dma = pltpu.SemaphoreType.DMA
    pieces, input_grad = pl.pallas_call(
        kernel,
        out_shape=(
            jax.ShapeDtypeStruct((3, 2, 4, 32, 1024), BF),
            jax.ShapeDtypeStruct((512, 128), BF),
        ),
        in_specs=[smem] * 3 + [hbm] * 5,
        out_specs=(vmem, vmem),
        scratch_shapes=[
            pltpu.VMEM((3, 128, 2048), F32),
            pltpu.VMEM((512, 4096), BF),
            pltpu.VMEM((3, 2, 4, 32, 1024), BF),
            pltpu.VMEM((32, 2, 32, 128), BF),
            pltpu.VMEM((32, 2, 32, 128), BF),
            pltpu.VMEM((32, 2, 32, 128), BF),
            pltpu.VMEM((1024, 2048), BF),
            pltpu.VMEM((512, 1024), BF),
            pltpu.VMEM((512, 512), BF),
            pltpu.VMEM((512, 2048), F32),
            pltpu.VMEM((512, 2048), BF),
            pltpu.VMEM((NC, 2, RR, 2048), BF),
            pltpu.VMEM((NC, 2, 2, RR, 2048), BF),
            pltpu.VMEM((512, 2048), BF),
            pltpu.VMEM((NC, 32, 3, RR, 128), BF),
            [pltpu.VMEM((32, 3, RR, 128), BF)] * NC,
            pltpu.VMEM((2, 4, 2, 2, 32, 512), CT),
            pltpu.VMEM((2, 4, 2, 32, 512), CT),
            pltpu.VMEM((2, 4, 2, 32, 512), BF),
            pltpu.VMEM((16, 32, 512), BF),
            dma((4,)), dma((2, 4)), dma((2, 4)), dma((2,)), dma((2,)), dma((2,)), dma((2,)),
            dma((3, 32)), dma((3, 32)), dma((12,)), dma((12,)), dma((4,)), dma((4,)),
            dma((NC, 6)), dma((NC, 6)), dma((NC, 32)), dma((NC, 32)),
            dma((2,)), dma((2,)), dma((2, 4, 2)), dma((16,)),
        ],
        compiler_params=pltpu.CompilerParams(
            collective_id=0, has_side_effects=True, vmem_limit_bytes=56 * 1024 * 1024
        ),
        cost_estimate=pl.CostEstimate(flops=4 * 2**30, bytes_accessed=12 * 2**20, transcendentals=2**18),
    )(
        inverse, new_map, counts,
        old_master.reshape(128, 2048), old_moment.reshape(128, 2048), old_second.reshape(128, 2048),
        tokens_in, upstream,
    )
    pieces = pieces.reshape(3, 1, 1, 256, 1024).astype(F32)
    return pieces[0], pieces[1], pieces[2], input_grad


def solution(mesh):
    pieces = P("tensor", "dp", None, None)
    return jax.shard_map(
        shards,
        mesh=mesh,
        in_specs=(pieces, pieces, pieces, P("dp", None), P("dp", "tensor"), P(), P(), P()),
        out_specs=(pieces, pieces, pieces, P("dp", "tensor")),
        check_vma=False,
    )
```

time: 160 us -> 142 us (0.89); the launches traced: 160 us -> 140 us
  Pallas kernels: 154 us -> 134 us
    pallas_call x1, Pallas kernels: 154 us -> 134 us  [shards(): pl.pallas_call(kernel, out_shape=(jax.ShapeDtypeStruct((3, 2, 4, 32, 1024...]
where the time goes in v3:
time: 142 us; the launch traced here: 140 us
  Pallas kernels  134 us (94%)
  local copies, waits for them, and re-layouts  3.83 us (3%)
    pallas_call x1, Pallas kernels, shards(): pl.pallas_call(kernel, out_shape=(jax.ShapeDtypeStruct((3, 2, 4, 32, 1024...  134 us
    slice x1, local copies, waits for them, and re-layouts, shards(): return (pieces[0], pieces[1], pieces[2], input_grad)  3.17 us

profile of v3, /device:TPU:1, one launch (start us, length us, event | category | flops | bytes accessed | tf_op | source)
XLA Modules:
  0.0 140.1 jit_solution(3343931724701532888)
XLA Ops:
  0.6 1.3 select_reduce_fusion.inv_ref
  1.9 134.4 %shard_map.111 = (bf16[3,2,4,32,1024]{4,3,2,1,0:T(8,128)(2,1)}, bf16[512,128]{1,0:T(8,128)(2,1)}) custom-call(s32[32]{0:T(128)} %select_reduce_fusion.inv_ref, s32[32]{0:T(128)} %new_ref.1, s32[8]{0:T(128)} %cnt_ref.1, f32[128,2048]{1,0:T(8,128)} %bitcast.9, f32[128,2048]{1,0:T(8,128)} %bitcast.10, f32[128,2048]{1,0:T(8,128)} %bitcast.11, ...), custom_call_target="tpu_custom_call" | custom-call | flops 4294967296 | bytes 12582912 | tf_op jit(solution)/shard_map/pallas_call | solution.py:487
  136.3 0.0 copy-start
  136.3 3.2 %fusion = (f32[1,2,4,32,1024]{4,3,2,1,0:T(8,128)}, f32[1,2,4,32,1024]{4,3,2,1,0:T(8,128)}, f32[1,2,4,32,1024]{4,3,2,1,0:T(8,128)}) fusion(bf16[3,2,4,32,1024]{4,3,2,1,0:T(8,128)(2,1)} %get-tuple-element.6), kind=kLoop, calls=%fused_computation.2 | loop fusion | bytes 6291456 | tf_op jit(solution)/shard_map/slice | solution.py:531
  139.5 0.0 copy-done
  139.5 0.7 copy.13
Async XLA Ops:
  136.3 3.2 %copy-start = (bf16[512,128]{1,0:T(8,128)(2,1)S(1)}, bf16[512,128]{1,0:T(8,128)(2,1)}, u32[]{:S(2)}) copy-start(bf16[512,128]{1,0:T(8,128)(2,1)} %get-tuple-element.18) | copy-start | bytes 393220

commit v4 on v3

--- a/solution.py
+++ b/solution.py
@@ -14,16 +14,16 @@
 BF = jnp.bfloat16
 F32 = jnp.float32
 NT = (((1,), (1,)), ((), ()))
-NC = 4
+NC = 2
 PER = NC // 2
 RR = 32 // PER
 CT = F32
 
 
 def kernel(
-    inv_ref, new_ref, cnt_ref, om_ref, oo_ref, os_ref, tok_ref, up_ref,
+    map_ref, new_ref, cnt_ref, om_ref, oo_ref, os_ref, tok_ref, up_ref,
     out_ref, ig_ref,
-    old, tok, send1, spread_a, spread_b, spread_c, gath, lhs, tsend, acc, part, r1, r2, wg,
+    inv_ref, old, tok, send1, spread_a, spread_b, spread_c, gath, lhs, tsend, acc, part, r1, r2, wg,
     upd, send2, cpart, crecv, csum, cfin,
     ld, us, ur, es, er, ts, tr, p1s, p1r, xs, xr, ws, wr, rs, rr, p2s, p2r, ks, kr, cs, cr,
 ):
@@ -48,6 +48,9 @@
     def cols(index, width):
         return pl.ds(pl.multiple_of(index * width, width), width)
 
+    def spread_out(n):
+        return (n % 4) * 8 + n // 4
+
     sent = []
 
     def start(*copies):
@@ -87,34 +90,40 @@
 
         lax.fori_loop(0, 8, body, 0)
 
-    def half(zz, h):
-        return pl.ds(pl.multiple_of(zz * 512 + h * 256, 256), 256)
-
-    def u1(h, dz):
+    near = 1 + 2 * zl
+    z_near, z_other, z_far = (z + 4 - near) % 4, (z + near) % 4, (z + 2) % 4
+    own_blocks = ((zl, z), (zl, z_near), (zp, z_near), (zp, z_far))
+    pair_blocks = ((zp, z), (zp, z_other), (zl, z_other), (zl, z_far))
+
+    def place_of(zz, zs, xx):
+        return gath.at[cols(zz, 512), cols(xx * 4 + zs, 128)]
+
+    def u1(dz):
         to = (z + dz) % 4
+        lo, at = {1: (0, 1 + zl), 3: (1, 2 - zl), 2: (zp, 3)}[dz]
         return remote(
-            up_ref.at[pl.ds(h * 256, 256), cols(to, 128)], gath.at[half(zl, h), cols(x * 4 + z, 128)],
-            us.at[h, dz], ur.at[h, dz], g, to * 8 + x * 2 + k,
+            up_ref.at[:, cols(to, 128)], place_of(zl, z, x), us.at[dz], ur.at[at], lo * 4 + y, to * 8 + x * 2 + k
         )
 
-    def u1_in(h, dz):
-        of = (z + 4 - dz) % 4
-        return remote(
-            up_ref.at[pl.ds(h * 256, 256), cols(z, 128)], gath.at[half(zl, h), cols(x * 4 + of, 128)],
-            us.at[h, dz], ur.at[h, dz], g, t_core,
-        )
-
-    def u1_wait(h):
-        if h == 0:
-            u1_own.wait()
-        for dz in (1, 2, 3):
-            u1_in(h, dz).wait_recv()
-
-    u1_own = pltpu.make_async_copy(up_ref.at[:, cols(z, 128)], gath.at[cols(zl, 512), cols(x * 4 + z, 128)], ur.at[0, 0])
-
-    def u2(zz, h):
-        ref = gath.at[half(zz, h), cols(x, 512)]
-        return remote(ref, ref, es.at[h], er.at[h], g_pair, t)
+    def u1_in(n):
+        return remote(up_ref.at[:, cols(z, 128)], place_of(*own_blocks[n], x), us.at[n], ur.at[n], g, t_core)
+
+    u1_own = pltpu.make_async_copy(up_ref.at[:, cols(z, 128)], place_of(zl, z, x), ur.at[0])
+
+    def u2(n):
+        ref = place_of(*own_blocks[n], x)
+        return remote(ref, ref, es.at[n], er.at[n], g_pair, t)
+
+    def u2_in(n):
+        ref = place_of(*pair_blocks[n], x)
+        return remote(ref, ref, es.at[n], er.at[n], g_pair, t)
+
+    def invert(piece, c):
+        slot = jnp.int32(0)
+        for s in range(1, 32):
+            slot = jnp.where(map_ref[s] == piece, jnp.int32(s), slot)
+        inv_ref[piece] = slot
+        return c
 
     def p1(a, j):
         p = (t + j) % 32
@@ -136,8 +145,8 @@
     def p1_start(a):
         p1_own(a).start()
 
-        def body(j, c):
-            p1(a, j).start()
+        def body(n, c):
+            p1(a, spread_out(n)).start()
             return c
 
         lax.fori_loop(1, 32, body, 0)
@@ -176,10 +185,39 @@
         ref = lhs.at[cols(kk, 256), cols(zp, 512)]
         return remote(ref, ref, ts.at[1], tr.at[1], g, t_core)
 
-    def ring_x(zz, block, h, way, sem):
-        ref = gath.at[half(zz, h), cols(block, 512)]
-        at = sem if zz is zl else 6 + sem
-        return remote(ref, ref, xs.at[at], xr.at[at], g, way)
+    blocks = own_blocks + pair_blocks
+
+    def x_copy(n, xx, rows, way, sem):
+        zz, zs = blocks[n]
+        ref = gath.at[pl.ds(pl.multiple_of(zz * 512 + rows[0], 256), rows[1]), cols(xx * 4 + zs, 128)]
+        return remote(ref, ref, xs.at[n, sem], xr.at[n, sem], g, way)
+
+    whole, top, bottom = (0, 512), (0, 256), (256, 256)
+
+    def x_near(n):
+        start(x_copy(n, x, whole, t_xup, 0), x_copy(n, x, whole, t_xdn, 1))
+
+    def x_relay(n):
+        x_copy(n, x_dn, whole, t_xup, 0).wait_recv()
+        start(x_copy(n, x_dn, top, t_xup, 2))
+        x_copy(n, x_up, whole, t_xdn, 1).wait_recv()
+        start(x_copy(n, x_up, bottom, t_xdn, 3))
+
+    def x_wait(n):
+        x_copy(n, x_far, top, t_xup, 2).wait_recv()
+        x_copy(n, x_far, bottom, t_xdn, 3).wait_recv()
+
+    def own_in(n):
+        if n == 0:
+            u1_own.wait()
+        else:
+            u1_in(n).wait_recv()
+        start(u2(n))
+        x_near(n)
+
+    def pair_in(n):
+        u2_in(n).wait_recv()
+        x_near(4 + n)
 
     def place(q):
         zs, half = q % 4, q // 4
@@ -228,12 +266,8 @@
         return sum_copy(i, 4 + so1, block(i, y_dn, so1), r2.at[i, 1, so1], g_dn)
 
     def add_into(i, yy, so1):
-        def body(c, carry):
-            at = (cols(i * 8 + yy * 2 + so1, RR), cols(c, 512))
-            part[at] = (part[at].astype(F32) + r1[i, so1, :, cols(c, 512)].astype(F32)).astype(BF)
-            return carry
-
-        lax.fori_loop(0, 4, body, 0)
+        at = cols(i * 8 + yy * 2 + so1, RR)
+        part[at, :] = (part[at, :].astype(F32) + r1[i, so1].astype(F32)).astype(BF)
 
     def sum_first(i):
         start(far_up(i), far_dn(i), near_up(i, 1), near_dn(i, 0))
@@ -256,27 +290,30 @@
             near_dn(i, so1).wait_recv()
         so0, r0 = i // PER, (i % PER) * RR
 
-        def body(q, carry):
-            bo, c10 = place(q)
-            here = cols(q, 128)
-            for so1 in range(2):
-                slot = inv_ref[bo * 4 + so1 * 2 + so0]
-                mine = cols(i * 8 + y * 2 + so1, RR)
-                grad = part[mine, here].astype(F32) + r2[i, 0, so1, :, here].astype(F32)
-                grad = grad + r2[i, 1, so1, :, here].astype(F32)
-                grad = grad * scale
-                rows = slice(r0, r0 + RR)
-                master = spread[0][slot, c10, rows].astype(F32)
-                moment = beta_first * spread[1][slot, c10, rows].astype(F32) + (1.0 - beta_first) * grad
-                second = beta_second * spread[2][slot, c10, rows].astype(F32) + (1.0 - beta_second) * grad * grad
-                update = moment / fix_first / (jnp.sqrt(second / fix_second) + epsilon) + decay_rate * master
-                piece = (bo * 2 + c10) * 2 + so1
-                upd[i, piece, 0] = (master - learn_rate * update).astype(BF)
-                upd[i, piece, 1] = moment.astype(BF)
-                upd[i, piece, 2] = second.astype(BF)
-            return carry
-
-        lax.fori_loop(0, 16, body, 0)
+        def body(zs, carry):
+            done = []
+            for xs in range(4):
+                bo, c10 = zs * 2 + xs // 2, xs % 2
+                here = cols(xs * 4 + zs, 128)
+                for so1 in range(2):
+                    slot = inv_ref[bo * 4 + so1 * 2 + so0]
+                    mine = cols(i * 8 + y * 2 + so1, RR)
+                    grad = part[mine, here].astype(F32) + r2[i, 0, so1, :, here].astype(F32)
+                    grad = (grad + r2[i, 1, so1, :, here].astype(F32)) * scale
+                    rows = slice(r0, r0 + RR)
+                    master = spread[0][slot, c10, rows].astype(F32)
+                    moment = beta_first * spread[1][slot, c10, rows].astype(F32) + (1.0 - beta_first) * grad
+                    second = beta_second * spread[2][slot, c10, rows].astype(F32) + (1.0 - beta_second) * grad * grad
+                    root = jnp.sqrt(second * (1.0 / fix_second)) + epsilon
+                    update = moment * (1.0 / fix_first) / root + decay_rate * master
+                    piece = (bo * 2 + c10) * 2 + so1
+                    done.append((piece, master - learn_rate * update, moment, second))
+            for piece, *values in done:
+                for a, value in enumerate(values):
+                    upd[i, piece, a] = value.astype(BF)
+            return carry
+
+        lax.fori_loop(0, 4, body, 0)
 
     def p2_place(i, px, pk, pz):
         return out_ref.at[:, i // PER, px, pl.ds((i % PER) * RR, RR), cols(pk * 4 + pz, 128)]
@@ -295,14 +332,18 @@
         return pltpu.make_async_copy(send2[i].at[t], p2_place(i, x, k, z), p2r.at[i, 0])
 
     def p2_start(i):
-        def body(j, carry):
-            p = (t + j) % 32
-            send2[i][p] = upd[i, new_ref[p]]
-            p2(i, j).start()
+        def select(j, carry):
+            for u in range(4):
+                send2[i][j * 4 + u] = upd[i, new_ref[j * 4 + u]]
+            return carry
+
+        lax.fori_loop(0, 8, select, 0)
+
+        def body(n, carry):
+            p2(i, spread_out(n)).start()
             return carry
 
         lax.fori_loop(1, 32, body, 0)
-        send2[i][t] = upd[i, new_ref[t]]
         p2_own(i).start()
 
     def back(tz):
@@ -365,77 +406,69 @@
     narrow(0)
     pl.semaphore_wait(barrier, 49)
     u1_own.start()
-    for h in range(2):
-        for dz in (2, 1, 3):
-            start(u1(h, dz))
+    for dz in (2, 1, 3):
+        start(u1(dz))
+    own_in(0)
+    narrow(1)
+    narrow(2)
+    own_in(1)
+    p1_start(0)
+    own_in(2)
+    own_in(3)
+    p1_start(1)
     loads[3].wait()
     lax.fori_loop(0, 4, transpose_tokens, 0)
-    narrow(1)
-    narrow(2)
-    u1_wait(0)
-    start(ring_x(zl, x, 0, t_xup, 0), u2(zl, 0))
-    p1_start(0)
-    u1_wait(1)
-    start(ring_x(zl, x, 1, t_xdn, 1), u2(zl, 1), ring_x(zl, x, 1, t_xup, 2), ring_x(zl, x, 0, t_xdn, 3))
     start(tokens_pair(zl, k))
-    ring_x(zl, x_dn, 0, t_xup, 0).wait_recv()
-    start(ring_x(zl, x_dn, 0, t_xup, 4))
-    ring_x(zl, x_up, 1, t_xdn, 1).wait_recv()
-    start(ring_x(zl, x_up, 1, t_xdn, 5))
-    u2(zp, 0).wait_recv()
-    start(ring_x(zp, x, 0, t_xup, 0))
-    u2(zp, 1).wait_recv()
-    start(ring_x(zp, x, 1, t_xdn, 1), ring_x(zp, x, 1, t_xup, 2), ring_x(zp, x, 0, t_xdn, 3))
-    p1_start(1)
+    x_relay(0)
+    x_relay(1)
+    pair_in(2)
+    pair_in(3)
+    lax.fori_loop(0, 32, invert, 0)
     p1_wait(0)
     lax.fori_loop(0, 16, weights, 0)
     start(ring_w(y, 0, 128, g_up, 0), ring_w(y, 0, 128, g_dn, 1))
     p1_start(2)
+    pair_in(0)
+    pair_in(1)
+    x_relay(2)
+    x_relay(3)
+    x_relay(6)
+    x_relay(7)
     tokens_pair(zp, k).wait_recv()
     start(tokens_core(k))
-    ring_x(zp, x_dn, 0, t_xup, 0).wait_recv()
-    start(ring_x(zp, x_dn, 0, t_xup, 4))
-    ring_x(zp, x_up, 1, t_xdn, 1).wait_recv()
-    start(ring_x(zp, x_up, 1, t_xdn, 5))
     ring_w(y_dn, 0, 128, g_up, 0).wait_recv()
     start(ring_w(y_dn, 0, 64, g_up, 2))
     ring_w(y_up, 0, 128, g_dn, 1).wait_recv()
     start(ring_w(y_up, 64, 64, g_dn, 3))
-    ring_x(zl, x_dn, 1, t_xup, 2).wait_recv()
-    ring_x(zl, x_up, 0, t_xdn, 3).wait_recv()
-    ring_x(zl, x_far, 0, t_xup, 4).wait_recv()
-    ring_x(zl, x_far, 1, t_xdn, 5).wait_recv()
+    x_relay(4)
+    x_relay(5)
+    x_wait(0)
+    x_wait(1)
+    x_wait(6)
+    x_wait(7)
     partial(zl)
     ring_w(y_far, 0, 64, g_up, 2).wait_recv()
     ring_w(y_far, 64, 64, g_dn, 3).wait_recv()
     back_send(zl)
-    back_sum(zl)
-    ring_x(zp, x_dn, 1, t_xup, 2).wait_recv()
-    ring_x(zp, x_up, 0, t_xdn, 3).wait_recv()
-    ring_x(zp, x_far, 0, t_xup, 4).wait_recv()
-    ring_x(zp, x_far, 1, t_xdn, 5).wait_recv()
+    x_wait(2)
+    x_wait(3)
+    x_wait(4)
+    x_wait(5)
     tokens_core(1 - k).wait_recv()
     partial(zp)
     sum_first(0)
+    back_sum(zl)
+    sum_second(0)
     sum_first(1)
-    back_send(zp)
-    sum_second(0)
-    sum_first(2)
-    sum_second(1)
-    sum_first(3)
     p1_wait(1)
     p1_wait(2)
     adamw(0)
     p2_start(0)
+    back_send(zp)
+    sum_second(1)
     back_sum(zp)
-    sum_second(2)
     adamw(1)
     p2_start(1)
-    sum_second(3)
-    adamw(2)
-    p2_start(2)
-    adamw(3)
-    p2_start(3)
 
     def c_wait(j, carry):
         remote(csum.at[0, 0, 0], cfin.at[j], cs.at[0, 0, 0], cr.at[j], g, t_core).wait_recv()
@@ -443,11 +476,11 @@
 
     lax.fori_loop(0, 16, c_wait, 0)
     token = lax.broadcasted_iota(jnp.int32, (512, 128), 0)
-    blocks = []
+    sums = []
     for xx in range(4):
         total = cfin[xx].astype(F32) + cfin[4 + xx].astype(F32)
-        blocks.append(total + cfin[8 + xx].astype(F32) + cfin[12 + xx].astype(F32))
-    full = jnp.concatenate(blocks, axis=0) * scale
+        sums.append(total + cfin[8 + xx].astype(F32) + cfin[12 + xx].astype(F32))
+    full = jnp.concatenate(sums, axis=0) * scale
     ig_ref[...] = jnp.where(token < live, full.T, 0.0).astype(BF)
 
     for i in range(NC):
@@ -478,8 +511,6 @@
 
 
 def shards(old_master, old_moment, old_second, tokens_in, upstream, counts, old_map, new_map):
-    slots = jnp.arange(32, dtype=jnp.int32)
-    inverse = jnp.sum(jnp.where(old_map[None, :] == slots[:, None], slots[None, :], 0), axis=1)
     hbm = pl.BlockSpec(memory_space=pl.ANY)
     smem = pl.BlockSpec(memory_space=pltpu.SMEM)
     vmem = pl.BlockSpec(memory_space=pltpu.VMEM)
@@ -493,6 +524,7 @@
         in_specs=[smem] * 3 + [hbm] * 5,
         out_specs=(vmem, vmem),
         scratch_shapes=[
+            pltpu.SMEM((32,), jnp.int32),
             pltpu.VMEM((3, 128, 2048), F32),
             pltpu.VMEM((512, 4096), BF),
             pltpu.VMEM((3, 2, 4, 32, 1024), BF),
@@ -513,8 +545,8 @@
             pltpu.VMEM((2, 4, 2, 32, 512), CT),
             pltpu.VMEM((2, 4, 2, 32, 512), BF),
             pltpu.VMEM((16, 32, 512), BF),
-            dma((4,)), dma((2, 4)), dma((2, 4)), dma((2,)), dma((2,)), dma((2,)), dma((2,)),
-            dma((3, 32)), dma((3, 32)), dma((12,)), dma((12,)), dma((4,)), dma((4,)),
+            dma((4,)), dma((4,)), dma((4,)), dma((4,)), dma((4,)), dma((2,)), dma((2,)),
+            dma((3, 32)), dma((3, 32)), dma((8, 4)), dma((8, 4)), dma((4,)), dma((4,)),
             dma((NC, 6)), dma((NC, 6)), dma((NC, 32)), dma((NC, 32)),
             dma((2,)), dma((2,)), dma((2, 4, 2)), dma((16,)),
         ],
@@ -523,7 +555,7 @@
         ),
         cost_estimate=pl.CostEstimate(flops=4 * 2**30, bytes_accessed=12 * 2**20, transcendentals=2**18),
     )(
-        inverse, new_map, counts,
+        old_map, new_map, counts,
         old_master.reshape(128, 2048), old_moment.reshape(128, 2048), old_second.reshape(128, 2048),
         tokens_in, upstream,
     )

time: 142 us -> 140 us (0.986)
  no operation moved by 1% of the time
where the time goes in v4:
time: 140 us; the launch traced here: 139 us
  Pallas kernels  135 us (96%)
  local copies, waits for them, and re-layouts  3.83 us (3%)
    pallas_call x1, Pallas kernels, shards(): pl.pallas_call(kernel, out_shape=(jax.ShapeDtypeStruct((3, 2, 4, 32, 1024...  135 us
    slice x1, local copies, waits for them, and re-layouts, shards(): return (pieces[0], pieces[1], pieces[2], input_grad)  3.17 us

profile of v4, /device:TPU:1, one launch (start us, length us, event | category | flops | bytes accessed | tf_op | source)
XLA Modules:
  0.0 139.1 jit_solution(18369138682991091919)
XLA Ops:
  0.6 134.6 %shard_map.111 = (bf16[3,2,4,32,1024]{4,3,2,1,0:T(8,128)(2,1)}, bf16[512,128]{1,0:T(8,128)(2,1)}) custom-call(s32[32]{0:T(128)} %map_ref.1, s32[32]{0:T(128)} %new_ref.1, s32[8]{0:T(128)} %cnt_ref.1, f32[128,2048]{1,0:T(8,128)} %bitcast.9, f32[128,2048]{1,0:T(8,128)} %bitcast.10, f32[128,2048]{1,0:T(8,128)} %bitcast.11, bf16[512,4096]{1,0:T(8,128)(2,1)} %tok_ref.1, ...), custom_call_target="tpu_custom_call" | custom-call | flops 4294967296 | bytes 12582912 | tf_op jit(solution)/shard_map/pallas_call | solution.py:518
  135.2 0.0 copy-start
  135.2 3.2 %fusion = (f32[1,2,4,32,1024]{4,3,2,1,0:T(8,128)}, f32[1,2,4,32,1024]{4,3,2,1,0:T(8,128)}, f32[1,2,4,32,1024]{4,3,2,1,0:T(8,128)}) fusion(bf16[3,2,4,32,1024]{4,3,2,1,0:T(8,128)(2,1)} %get-tuple-element.6), kind=kLoop, calls=%fused_computation | loop fusion | bytes 6291456 | tf_op jit(solution)/shard_map/slice | solution.py:563
  138.4 0.0 copy-done
  138.4 0.7 copy.13
Async XLA Ops:
  135.2 3.2 %copy-start = (bf16[512,128]{1,0:T(8,128)(2,1)S(1)}, bf16[512,128]{1,0:T(8,128)(2,1)}, u32[]{:S(2)}) copy-start(bf16[512,128]{1,0:T(8,128)(2,1)} %get-tuple-element.18) | copy-start | bytes 393220

commit v5 on v4

--- a/solution.py
+++ b/solution.py
@@ -415,7 +415,6 @@
     p1_start(0)
     own_in(2)
     own_in(3)
-    p1_start(1)
     loads[3].wait()
     lax.fori_loop(0, 4, transpose_tokens, 0)
     start(tokens_pair(zl, k))
@@ -423,12 +422,13 @@
     x_relay(1)
     pair_in(2)
     pair_in(3)
+    p1_start(1)
     lax.fori_loop(0, 32, invert, 0)
     p1_wait(0)
     lax.fori_loop(0, 16, weights, 0)
     start(ring_w(y, 0, 128, g_up, 0), ring_w(y, 0, 128, g_dn, 1))
+    pair_in(0)
     p1_start(2)
-    pair_in(0)
     pair_in(1)
     x_relay(2)
     x_relay(3)
@@ -457,16 +457,16 @@
     tokens_core(1 - k).wait_recv()
     partial(zp)
     sum_first(0)
+    back_send(zp)
     back_sum(zl)
     sum_second(0)
     sum_first(1)
     p1_wait(1)
     p1_wait(2)
+    back_sum(zp)
     adamw(0)
     p2_start(0)
-    back_send(zp)
     sum_second(1)
-    back_sum(zp)
     adamw(1)
     p2_start(1)
 

time: 140 us -> 135 us (0.964)
  Pallas kernels: 135 us -> 131 us
    pallas_call x1, Pallas kernels: 135 us -> 131 us  [shards(): pl.pallas_call(kernel, out_shape=(jax.ShapeDtypeStruct((3, 2, 4, 32, 1024...]
where the time goes in v5:
time: 135 us
  Pallas kernels  131 us (97%)
  local copies, waits for them, and re-layouts  3.83 us (3%)
    pallas_call x1, Pallas kernels, shards(): pl.pallas_call(kernel, out_shape=(jax.ShapeDtypeStruct((3, 2, 4, 32, 1024...  131 us
    slice x1, local copies, waits for them, and re-layouts, shards(): return (pieces[0], pieces[1], pieces[2], input_grad)  3.17 us

profile of v5, /device:TPU:1, one launch (start us, length us, event | category | flops | bytes accessed | tf_op | source)
XLA Modules:
  0.0 135.2 jit_solution(8541961089377090493)
XLA Ops:
  0.6 130.7 %shard_map.111 = (bf16[3,2,4,32,1024]{4,3,2,1,0:T(8,128)(2,1)}, bf16[512,128]{1,0:T(8,128)(2,1)}) custom-call(s32[32]{0:T(128)} %map_ref.1, s32[32]{0:T(128)} %new_ref.1, s32[8]{0:T(128)} %cnt_ref.1, f32[128,2048]{1,0:T(8,128)} %bitcast.9, f32[128,2048]{1,0:T(8,128)} %bitcast.10, f32[128,2048]{1,0:T(8,128)} %bitcast.11, bf16[512,4096]{1,0:T(8,128)(2,1)} %tok_ref.1, ...), custom_call_target="tpu_custom_call" | custom-call | flops 4294967296 | bytes 12582912 | tf_op jit(solution)/shard_map/pallas_call | solution.py:518
  131.4 0.0 copy-start
  131.4 3.2 %fusion = (f32[1,2,4,32,1024]{4,3,2,1,0:T(8,128)}, f32[1,2,4,32,1024]{4,3,2,1,0:T(8,128)}, f32[1,2,4,32,1024]{4,3,2,1,0:T(8,128)}) fusion(bf16[3,2,4,32,1024]{4,3,2,1,0:T(8,128)(2,1)} %get-tuple-element.6), kind=kLoop, calls=%fused_computation | loop fusion | bytes 6291456 | tf_op jit(solution)/shard_map/slice | solution.py:563
  134.6 0.0 copy-done
  134.6 0.7 copy.13
Async XLA Ops:
  131.4 3.2 %copy-start = (bf16[512,128]{1,0:T(8,128)(2,1)S(1)}, bf16[512,128]{1,0:T(8,128)(2,1)}, u32[]{:S(2)}) copy-start(bf16[512,128]{1,0:T(8,128)(2,1)} %get-tuple-element.18) | copy-start | bytes 393220

commit v6 on v5

--- a/solution.py
+++ b/solution.py
@@ -428,8 +428,8 @@
     lax.fori_loop(0, 16, weights, 0)
     start(ring_w(y, 0, 128, g_up, 0), ring_w(y, 0, 128, g_dn, 1))
     pair_in(0)
+    pair_in(1)
     p1_start(2)
-    pair_in(1)
     x_relay(2)
     x_relay(3)
     x_relay(6)

time: 135 us -> 135 us (level)
  no operation moved by 1% of the time
where the time goes in v6:
time: 135 us
  Pallas kernels  131 us (97%)
  local copies, waits for them, and re-layouts  3.83 us (3%)
    pallas_call x1, Pallas kernels, shards(): pl.pallas_call(kernel, out_shape=(jax.ShapeDtypeStruct((3, 2, 4, 32, 1024...  131 us
    slice x1, local copies, waits for them, and re-layouts, shards(): return (pieces[0], pieces[1], pieces[2], input_grad)  3.17 us

profile of v6, /device:TPU:1, one launch (start us, length us, event | category | flops | bytes accessed | tf_op | source)
XLA Modules:
  0.0 135.2 jit_solution(15626290794422059875)
XLA Ops:
  0.6 130.7 %shard_map.111 = (bf16[3,2,4,32,1024]{4,3,2,1,0:T(8,128)(2,1)}, bf16[512,128]{1,0:T(8,128)(2,1)}) custom-call(s32[32]{0:T(128)} %map_ref.1, s32[32]{0:T(128)} %new_ref.1, s32[8]{0:T(128)} %cnt_ref.1, f32[128,2048]{1,0:T(8,128)} %bitcast.9, f32[128,2048]{1,0:T(8,128)} %bitcast.10, f32[128,2048]{1,0:T(8,128)} %bitcast.11, bf16[512,4096]{1,0:T(8,128)(2,1)} %tok_ref.1, ...), custom_call_target="tpu_custom_call" | custom-call | flops 4294967296 | bytes 12582912 | tf_op jit(solution)/shard_map/pallas_call | solution.py:518
  131.4 0.0 copy-start
  131.4 3.2 %fusion = (f32[1,2,4,32,1024]{4,3,2,1,0:T(8,128)}, f32[1,2,4,32,1024]{4,3,2,1,0:T(8,128)}, f32[1,2,4,32,1024]{4,3,2,1,0:T(8,128)}) fusion(bf16[3,2,4,32,1024]{4,3,2,1,0:T(8,128)(2,1)} %get-tuple-element.6), kind=kLoop, calls=%fused_computation | loop fusion | bytes 6291456 | tf_op jit(solution)/shard_map/slice | solution.py:563
  134.6 0.0 copy-done
  134.6 0.7 copy.13
Async XLA Ops:
  131.4 3.2 %copy-start = (bf16[512,128]{1,0:T(8,128)(2,1)S(1)}, bf16[512,128]{1,0:T(8,128)(2,1)}, u32[]{:S(2)}) copy-start(bf16[512,128]{1,0:T(8,128)(2,1)} %get-tuple-element.18) | copy-start | bytes 393220
